TPU v7x, 32 devices: a whole 2x2x4 slice. The times are simulated.
32 devices in a mesh: req: 16 (over z, x, core), tp: 2 (over y).
Axes of the slice: x: 2, y: 2, z: 4, core: 2. Of those that a mesh axis runs over, the one named last changes fastest.
Arguments:
- gate_in: bfloat16 [2, 1024, 4096], P(None, 'req', 'tp'), may hold values from -6 to 6
- mix_in: bfloat16 [2, 1024, 4096], P(None, 'req', 'tp'), may hold values from -6 to 6
- keys_in: bfloat16 [2, 1024, 256], P(None, 'req'), may hold values from -6 to 6
- step_in: bfloat16 [2, 1024, 64], P(None, 'req', 'tp'), may hold values from -6 to 6
- resid_in: bfloat16 [2, 1024, 2048], P(None, 'req', 'tp'), may hold values from -12 to 12
- kernel_mix: float32 [2, 4, 4096], P(None, None, 'tp'), may hold values from -3 to 3
- kernel_keys: float32 [2, 4, 256], replicated, may hold values from -3 to 3
- step_bias: float32 [2, 64], P(None, 'tp'), may hold values from -4 to 0
- decay_rate: float32 [2, 64], P(None, 'tp'), may hold values from 0.02 to 2
- skip_gain: float32 [2, 64], P(None, 'tp'), may hold values from 0.5 to 1.5
- norm_gain: float32 [2, 4096], P(None, 'tp'), may hold values from 0.5 to 1.5
- final_gain: float32 [2, 2048], replicated, may hold values from 0.5 to 1.5
- out_weight: bfloat16 [2, 4096, 2048], P(None, 'tp', 'req'), may hold values from -0.09375 to 0.09375
- head_weight: bfloat16 [2, 25600, 2048], P(None, 'req'), may hold values from -8 to 8
- history_mix: bfloat16 [2, 48, 3, 4096], P(None, 'req', None, 'tp'), may hold values from -6 to 6
- history_keys: bfloat16 [2, 48, 3, 256], P(None, 'req'), may hold values from -6 to 6
- start_state: bfloat16 [2, 48, 4096, 128], P(None, 'req', 'tp'), may hold values from -0.59765625 to 0.59765625
- lengths: int32 [16, 3], P('req'), may hold values from 1 to 32, 64 in all within a row
- continued: int32 [16, 3], P('req'), may hold values 0 or 1
- targets: int32 [1024], P('req'), may hold values from 0 to 25599
- score_flag: int32 [1024], P('req'), may hold values 0 or 1
Outputs:
- logprobs: float32 [2, 1024], P(None, ('req', 'tp'))
Inputs may be any that keep to these rules, and one draw needn't show every extreme that they name: The 3 lengths of a row fill its 64 slots exactly.
All inputs are finite; a program needn't handle non-finite values. No bound on the sum of `continued` or of `score_flag` on one device may be relied on, other than what follows from the above.
Results may differ from a plain program's by a relative error of at most 0.00075.
Values may be sent and summed in bfloat16 or wider, within the bound.
A program may use at most 128 MiB of HBM per device.

v0:
```python
import jax
import jax.numpy as jnp
from jax import lax
from jax.sharding import PartitionSpec as P

EPSILON = 1e-05
PRECISE = lax.Precision.HIGHEST


def merged_2(part, axis, combine):
    gathered = jax.tree.map(lambda a: lax.all_gather(a, axis), part)

    def take(source):
        return jax.tree.map(lambda a: lax.dynamic_index_in_dim(a, source, 0, False), gathered)

    return lax.fori_loop(
        1, lax.axis_size(axis), lambda source, state: combine(state, take(source)), take(0)
    )


def request_layout(lengths, step_count):
    starts = jnp.cumsum(lengths) - lengths
    time_index = jnp.arange(step_count, dtype=jnp.int32)
    segment = jnp.sum((time_index[:, None] >= starts[None, 1:]).astype(jnp.int32), axis=1)
    member = segment[:, None] == jnp.arange(lengths.shape[0], dtype=jnp.int32)[None, :]
    first_step = jnp.sum(jnp.where(member, starts[None, :], 0), axis=1)
    return (starts, segment, member, time_index - first_step)


def causal_conv(stream, kernel, history, member, offset):
    tap_count = kernel.shape[0]
    history_len = tap_count - 1
    current = stream.astype(jnp.float32)
    member_bf = member.astype(jnp.bfloat16)
    slot_values = [
        jnp.dot(member_bf, history[:, slot_index, :], preferred_element_type=jnp.float32)
        for slot_index in range(history_len)
    ]
    output = kernel[history_len][None, :] * current
    for lag_steps in range(1, tap_count):
        shifted = jnp.concatenate(
            [jnp.zeros((lag_steps, current.shape[1]), current.dtype), current[:-lag_steps]], axis=0
        )
        earlier = jnp.zeros_like(current)
        for slot_index in range(history_len):
            earlier = earlier + jnp.where(
                (offset - lag_steps == slot_index - history_len)[:, None],
                slot_values[slot_index],
                0.0,
            )
        output = output + kernel[history_len - lag_steps][None, :] * jnp.where(
            (offset >= lag_steps)[:, None], shifted, earlier
        )
    return jax.nn.silu(output)


def mixer_block(
    gate_rows,
    mix_rows,
    keys_rows,
    step_raw,
    kernel_mix,
    kernel_keys,
    step_bias,
    decay_rate,
    skip_gain,
    history_mix,
    history_keys,
    start_state,
    lengths,
    continued,
):
    step_count = gate_rows.shape[0]
    head_count = step_raw.shape[1]
    inner_width = mix_rows.shape[1]
    head_size = inner_width // head_count
    states = start_state.shape[2]
    starts, segment, member, offset = request_layout(lengths, step_count)
    keep_state = continued.astype(jnp.bfloat16)
    mixed = causal_conv(
        mix_rows, kernel_mix, history_mix * keep_state[:, None, None], member, offset
    )
    projected = causal_conv(
        keys_rows, kernel_keys, history_keys * keep_state[:, None, None], member, offset
    )
    inject = projected[:, :states]
    readout = projected[:, states:]
    step_size = jax.nn.softplus(step_raw.astype(jnp.float32) + step_bias[None, :])
    log_decay = -step_size * decay_rate[None, :]
    running = jnp.cumsum(log_decay, axis=0)
    time_index = jnp.arange(step_count, dtype=jnp.int32)
    causal = (segment[:, None] == segment[None, :]) & (time_index[:, None] >= time_index[None, :])
    spread = jnp.minimum(running[:, None, :] - running[None, :, :], 0.0)
    transfer = jnp.where(causal[:, :, None], jnp.exp(spread), 0.0)
    intersection = jnp.dot(readout, inject.T, precision=PRECISE)
    kernel_full = transfer * intersection[:, :, None]
    values = mixed.reshape(step_count, head_count, head_size)
    output = jnp.einsum(
        "tsh,shp->thp", kernel_full, step_size[:, :, None] * values, precision=PRECISE
    )
    before = jnp.take(running - log_decay, starts, axis=0)
    member_float = member.astype(jnp.float32)
    entry_level = jnp.dot(member_float, before, precision=PRECISE)
    carried = jnp.exp(jnp.minimum(running - entry_level, 0.0))
    initial = start_state.astype(jnp.float32) * keep_state.astype(jnp.float32)[:, None, None]
    readings = jnp.einsum("tn,rcn->trc", readout, initial, precision=PRECISE)
    chosen = jnp.sum(member_float[:, :, None] * readings, axis=1).reshape(
        step_count, head_count, head_size
    )
    output = output + carried[:, :, None] * chosen + skip_gain[None, :, None] * values
    return output.reshape(step_count, inner_width) * jax.nn.silu(gate_rows.astype(jnp.float32))


def head_scores(head_weight, vocab_start, piece_rows):
    rows_hidden, rows_target = piece_rows
    logits = jnp.einsum(
        "mnd,mvd->mnv", rows_hidden, head_weight, preferred_element_type=jnp.float32
    )
    peak_logit = jnp.max(logits, axis=2)
    spread = jnp.sum(jnp.exp(logits - peak_logit[:, :, None]), axis=2)
    local_id = rows_target[0] - vocab_start
    matches = jnp.arange(head_weight.shape[1], dtype=jnp.int32)[None, :] == local_id[:, None]
    picked = jnp.sum(jnp.where(matches[None, :, :], logits, 0.0), axis=2)
    return (peak_logit, spread, picked)


def fold_stats(first_stats, second_stats):
    peak_logit = jnp.maximum(first_stats[0], second_stats[0])
    spread = first_stats[1] * jnp.exp(first_stats[0] - peak_logit) + second_stats[1] * jnp.exp(
        second_stats[0] - peak_logit
    )
    return (peak_logit, spread, first_stats[2] + second_stats[2])


def local(
    gate_in,
    mix_in,
    keys_in,
    step_in,
    resid_in,
    kernel_mix,
    kernel_keys,
    step_bias,
    decay_rate,
    skip_gain,
    norm_gain,
    final_gain,
    out_weight,
    head_weight,
    history_mix,
    history_keys,
    start_state,
    lengths,
    continued,
    targets,
    score_flag,
):
    groups = lax.axis_size("tp")
    shards = lax.axis_size("req")
    lane_index = lax.axis_index("tp")
    shard_index = lax.axis_index("req")
    models = gate_in.shape[0]
    step_count = gate_in.shape[1]
    row_count = step_count // groups
    gated = jnp.stack(
        [
            mixer_block(
                gate_in[model_index],
                mix_in[model_index],
                keys_in[model_index],
                step_in[model_index],
                kernel_mix[model_index],
                kernel_keys[model_index],
                step_bias[model_index],
                decay_rate[model_index],
                skip_gain[model_index],
                history_mix[model_index],
                history_keys[model_index],
                start_state[model_index],
                lengths[0],
                continued[0],
            )
            for model_index in range(models)
        ]
    )
    squares = lax.psum(jnp.sum(gated * gated, axis=2), "tp")
    inner_width = gated.shape[2] * groups
    normed = (
        gated * lax.rsqrt(squares / inner_width + EPSILON)[:, :, None] * norm_gain[:, None, :]
    ).astype(jnp.bfloat16)
    partial_out = jnp.einsum(
        "mtc,mcd->mtd",
        normed,
        lax.all_gather(out_weight, "req", axis=2, tiled=True),
        preferred_element_type=jnp.float32,
    )
    update = lax.psum_scatter(partial_out, "tp", scatter_dimension=2, tiled=True)
    hidden = (resid_in.astype(jnp.float32) + update).astype(jnp.bfloat16)
    part_width = hidden.shape[2]
    full_width = part_width * groups
    vocab_part = head_weight.shape[1]
    hidden_float = hidden.astype(jnp.float32)
    final_squares = lax.psum(jnp.sum(hidden_float * hidden_float, axis=2), "tp")
    gain_part = lax.dynamic_slice_in_dim(final_gain, lane_index * part_width, part_width, 1)
    final_rows = (
        hidden_float
        * lax.rsqrt(final_squares / full_width + EPSILON)[:, :, None]
        * gain_part[:, None, :]
    ).astype(jnp.bfloat16)
    every_rows, every_target = (
        lax.all_gather(final_rows, "req", axis=1, tiled=True),
        lax.all_gather(targets, "req", axis=0, tiled=True),
    )
    blocks = every_rows.reshape(models, shards, groups, row_count, part_width)
    regrouped = lax.all_to_all(blocks, "tp", split_axis=2, concat_axis=4, tiled=True).reshape(
        models, shards * row_count, full_width
    )
    target_rows = lax.dynamic_slice_in_dim(
        every_target.reshape(shards, groups, row_count), lane_index, 1, 1
    ).reshape(1, shards * row_count)
    statistics = head_scores(head_weight, shard_index * vocab_part, (regrouped, target_rows))
    merged = merged_2(statistics, "req", fold_stats)
    peak_logit = lax.dynamic_slice_in_dim(merged[0], shard_index * row_count, row_count, 1)
    spread = lax.dynamic_slice_in_dim(merged[1], shard_index * row_count, row_count, 1)
    picked = lax.dynamic_slice_in_dim(merged[2], shard_index * row_count, row_count, 1)
    scored_rows = lax.dynamic_slice_in_dim(score_flag, lane_index * row_count, row_count, 0).astype(
        jnp.float32
    )
    return (picked - (peak_logit + jnp.log(spread))) * scored_rows[None, :]


def solution(mesh):
    placed = (
        P(None, "req", "tp"),
        P(None, "req", "tp"),
        P(None, "req", None),
        P(None, "req", "tp"),
        P(None, "req", "tp"),
        P(None, None, "tp"),
        P(),
        P(None, "tp"),
        P(None, "tp"),
        P(None, "tp"),
        P(None, "tp"),
        P(),
        P(None, "tp", "req"),
        P(None, "req", None),
        P(None, "req", None, "tp"),
        P(None, "req", None, None),
        P(None, "req", "tp", None),
        P("req", None),
        P("req", None),
        P("req"),
        P("req"),
    )
    return jax.shard_map(
        local, mesh=mesh, in_specs=placed, out_specs=P(None, ("req", "tp")), check_vma=False
    )
```

profile of v0, /device:TPU:0, one launch (start us, length us, event | category | flops | bytes accessed | tf_op | source)
XLA Modules:
  0.0 393.3 jit_solution(5759660883840986590)
XLA Ops:
  12.4 1.6 fusion.165
  22.1 5.0 %fusion.12 = f32[64,2048]{1,0:T(8,128)S(1)} fusion(bf16[2,3,2048,128]{3,2,1,0:T(8,128)(2,1)} %param.41, f32[3]{0:T(128)S(1)} %get-tuple-element.261, f32[64,3]{0,1:T(4,128)S(1)} %fusion.131, f32[64,256]{1,0:T(8,128)S(1)} %divide_multiply_fusion.2), kind=kOutput, calls=%fused_computation.23 | convolution fusion | flops 606208000 | bytes 2132480 | tf_op jit(solution)/shard_map/tn,rcn->trc/dot_general | solution.py:106
  30.0 2.1 fusion.15
  34.0 2.5 divide_multiply_fusion.1
  37.7 5.1 %fusion.13 = f32[64,2048]{1,0:T(8,128)S(1)} fusion(f32[3]{0:T(128)S(1)} %copy-done.51, bf16[2,3,2048,128]{3,2,1,0:T(8,128)(2,1)} %param.41, f32[64,3]{0,1:T(4,128)S(1)} %copy-done.12, f32[64,256]{1,0:T(8,128)S(1)} %divide_multiply_fusion.3), kind=kOutput, calls=%fused_computation.24 | convolution fusion | flops 606208000 | bytes 2132480 | tf_op jit(solution)/shard_map/tn,rcn->trc/dot_general | solution.py:106
  44.3 2.1 fusion.17
  46.7 1.5 fusion.37
  48.4 5.8 %psum.14 = f32[2,64]{1,0:T(2,128)S(1)} all-reduce(f32[2,64]{1,0:T(2,128)S(1)} %multiply_reduce_fusion), channel_id=1, replica_groups=mesh['req'=16,'tp'=2] {'tp'}, use_global_device_ids=true, to_apply=%region_8.10 | all-reduce | flops 128 | bytes 1024 | tf_op jit(solution)/shard_map/psum | solution.py:186
  54.2 88.4 %all-gather.9.cloned.1.call-done = bf16[2,2048,2048]{2,1,0:T(8,128)(2,1)} async-done(((bf16[2,2048,128]{2,1,0:T(8,128)(2,1)}), bf16[2,2048,2048]{2,1,0:T(8,128)(2,1)}) %all-gather.9.cloned.1.call-update) | async-done | bytes 16777232 | tf_op jit(solution)/shard_map/all_gather | solution.py:194
  142.6 9.8 %fusion.45 = f32[2,64,2048]{2,1,0:T(8,128)} fusion(bf16[2,2048,2048]{2,1,0:T(8,128)(2,1)} %all-gather.9.cloned.1.call-done, f32[1,64,2048]{2,1,0:T(8,128)S(1)} %get-tuple-element.209, f32[1,64,2048]{2,1,0:T(8,128)S(1)} %get-tuple-element.208, f32[2,2048]{1,0:T(2,128)S(1)} %copy-done.4, f32[2,64]{1,0:T(2,128)S(1)} %add_rsqrt_fusion.1), kind=kOutput, calls=%fused_computation.69 | convolution fusion | flops 1074790400 | bytes 18891264 | tf_op jit(solution)/shard_map/mtc,mcd->mtd/dot_general | solution.py:191
  152.5 18.6 %reduce-scatter.2.cloned.1.call-done = f32[2,64,1024]{2,1,0:T(8,128)} async-done(((f32[2,64,2048]{2,1,0:T(8,128)}), f32[2,64,1024]{2,1,0:T(8,128)}) %reduce-scatter.2.cloned.1.call-update) | async-done | bytes 524304 | tf_op jit(solution)/shard_map/reduce_scatter | solution.py:197
  172.3 4.9 %psum.15 = f32[2,64]{1,0:T(2,128)S(1)} all-reduce(f32[2,64]{1,0:T(2,128)S(1)} %fusion.42), channel_id=1, replica_groups=mesh['req'=16,'tp'=2] {'tp'}, use_global_device_ids=true, to_apply=%region_11.13 | all-reduce | flops 128 | bytes 1024 | tf_op jit(solution)/shard_map/psum | solution.py:203
  177.2 1.9 fusion.44
  179.1 50.7 %all-gather.11.cloned.1.call-done = bf16[2,1024,1024]{2,1,0:T(8,128)(2,1)} async-done(((bf16[2,64,1024]{2,1,0:T(8,128)(2,1)}), bf16[2,1024,1024]{2,1,0:T(8,128)(2,1)}) %all-gather.11.cloned.1.call-update) | async-done | bytes 4194320 | tf_op jit(solution)/shard_map/all_gather | solution.py:211
  229.9 5.0 %copy.110 = bf16[2,16,2,32,1024]{4,3,1,0,2:T(8,128)(2,1)} copy(bf16[2,16,2,32,1024]{4,3,2,1,0:T(8,128)(2,1)} %bitcast.246) | data formatting | bytes 8388608 | tf_op jit(solution)/shard_map/reshape | solution.py:214
  234.9 5.8 %all-to-all-start = ((bf16[2,16,2,32,1024]{4,3,1,0,2:T(8,128)(2,1)}), bf16[2,16,2,32,1024]{4,3,1,0,2:T(8,128)(2,1)}, u32[]{:S(2)}, u32[]{:S(2)}) async-start(bf16[2,16,2,32,1024]{4,3,1,0,2:T(8,128)(2,1)} %copy.110), calls=%async_computation.1 | async-start | bytes 8388608 | tf_op jit(solution)/shard_map/all_to_all | solution.py:215
  242.2 59.2 %all-reduce.13 = s32[16,2,32]{2,1,0:T(2,128)S(1)} all-reduce(s32[16,2,32]{2,1,0:T(2,128)S(1)} %reshape.343), channel_id=1, replica_groups=mesh['req'=16,'tp'=2] {'req'}, use_global_device_ids=true, to_apply=%add.12 | all-reduce | flops 1024 | bytes 8192
  302.2 8.6 %copy.111 = bf16[2,16,1,32,2,1024]{5,4,3,1,0,2:T(2,128)(2,1)} copy(bf16[2,16,1,32,2,1024]{5,3,1,0,4,2:T(8,128)(2,1)} %bitcast.63) | data formatting | bytes 8388608 | tf_op jit(solution)/shard_map/all_to_all | solution.py:215
  310.8 7.8 %reshape.342 = bf16[2,512,2048]{2,1,0:T(8,128)(2,1)} reshape(bf16[2,16,1,32,2,1024]{5,4,3,1,0,2:T(2,128)(2,1)} %copy.111) | data formatting | bytes 8388608 | tf_op jit(solution)/shard_map/reshape | solution.py:215
  318.6 11.1 %fusion.172 = (f32[2,512]{1,0:T(2,128)S(1)}, f32[2,512,1600]{1,2,0:T(8,128)S(1)}) fusion(bf16[2,512,2048]{2,1,0:T(8,128)(2,1)} %reshape.342, bf16[2,1600,2048]{2,1,0:T(8,128)(2,1)} %param.38), kind=kOutput, calls=%fused_computation.274 | convolution fusion | flops 6712523776 | bytes 23859200 | tf_op jit(solution)/shard_map/mnd,mvd->mnv/dot_general | solution.py:116
  329.6 1.6 select_reduce_fusion
  331.2 17.3 %all-gather.5 = f32[16,2,512]{2,1,0:T(2,128)S(1)} all-gather(f32[1,2,512]{2,1,0:T(2,128)S(1)} %bitcast.255), channel_id=4, replica_groups=mesh['req'=16,'tp'=2] {'req'}, dimensions={0}, use_global_device_ids=true | all-gather | bytes 69632 | tf_op jit(solution)/shard_map/all_gather | solution.py:11
  348.5 19.2 %all-gather.4 = f32[16,2,512]{2,1,0:T(2,128)S(1)} all-gather(f32[1,2,512]{2,1,0:T(2,128)S(1)} %bitcast.254), channel_id=3, replica_groups=mesh['req'=16,'tp'=2] {'req'}, dimensions={0}, use_global_device_ids=true | all-gather | bytes 69632 | tf_op jit(solution)/shard_map/all_gather | solution.py:11
  367.7 17.6 %all-gather.3 = f32[16,2,512]{2,1,0:T(2,128)S(1)} all-gather(f32[1,2,512]{2,1,0:T(2,128)S(1)} %bitcast.253), channel_id=2, replica_groups=mesh['req'=16,'tp'=2] {'req'}, dimensions={0}, use_global_device_ids=true | all-gather | bytes 69632 | tf_op jit(solution)/shard_map/all_gather | solution.py:11
  (207 shorter events, 26.0 us)
Async XLA Ops:
  6.5 146.0 %copy-start = (f32[2,2048]{1,0:T(2,128)S(1)}, f32[2,2048]{1,0:T(2,128)}, u32[]{:S(2)}) copy-start(f32[2,2048]{1,0:T(2,128)} %param.36) | copy-start | bytes 49156
  6.5 136.0 %all-gather.9.cloned.1.call-start = ((), (), s32[]{:S(2)}) async-start(), calls=%async_computation.2 | async-start | bytes 17825792 | tf_op jit(solution)/shard_map/all_gather | solution.py:194
  7.3 163.8 %reduce-scatter.2.cloned.1.call-start = ((), (), s32[]{:S(2)}) async-start(), calls=%async_computation.3 | async-start | bytes 1572864 | tf_op jit(solution)/shard_map/reduce_scatter | solution.py:197
  8.8 20.7 %copy-start.21 = (pred[3]{0:T(512)(128)(4,1)}, pred[3]{0:T(512)(128)(4,1)S(1)}, u32[]{:S(2)}) copy-start(pred[3]{0:T(512)(128)(4,1)S(1)} %get-tuple-element.205) | copy-start | bytes 13
  10.4 11.7 %copy-start.50 = (f32[3]{0:T(128)}, f32[3]{0:T(128)S(1)}, u32[]{:S(2)}) copy-start(f32[3]{0:T(128)S(1)} %get-tuple-element.261) | copy-start | bytes 40
  10.4 11.3 %copy-start.23 = (pred[64]{0:T(512)(128)(4,1)}, pred[64]{0:T(512)(128)(4,1)S(1)}, u32[]{:S(2)}) copy-start(pred[64]{0:T(512)(128)(4,1)S(1)} %get-tuple-element.263) | copy-start | bytes 196
  10.4 11.3 %copy-start.25 = (pred[64]{0:T(512)(128)(4,1)}, pred[64]{0:T(512)(128)(4,1)S(1)}, u32[]{:S(2)}) copy-start(pred[64]{0:T(512)(128)(4,1)S(1)} %get-tuple-element.264) | copy-start | bytes 196
  10.4 11.3 %copy-start.27 = (pred[64]{0:T(512)(128)(4,1)}, pred[64]{0:T(512)(128)(4,1)S(1)}, u32[]{:S(2)}) copy-start(pred[64]{0:T(512)(128)(4,1)S(1)} %get-tuple-element.265) | copy-start | bytes 196
  10.4 11.3 %copy-start.29 = (pred[64]{0:T(512)(128)(4,1)}, pred[64]{0:T(512)(128)(4,1)S(1)}, u32[]{:S(2)}) copy-start(pred[64]{0:T(512)(128)(4,1)S(1)} %get-tuple-element.266) | copy-start | bytes 196
  10.4 11.3 %copy-start.31 = (pred[64]{0:T(512)(128)(4,1)}, pred[64]{0:T(512)(128)(4,1)S(1)}, u32[]{:S(2)}) copy-start(pred[64]{0:T(512)(128)(4,1)S(1)} %get-tuple-element.267) | copy-start | bytes 196
  10.4 11.3 %copy-start.33 = (pred[64]{0:T(512)(128)(4,1)}, pred[64]{0:T(512)(128)(4,1)S(1)}, u32[]{:S(2)}) copy-start(pred[64]{0:T(512)(128)(4,1)S(1)} %get-tuple-element.268) | copy-start | bytes 196
  10.4 11.3 %copy-start.35 = (pred[64]{0:T(512)(128)(4,1)}, pred[64]{0:T(512)(128)(4,1)S(1)}, u32[]{:S(2)}) copy-start(pred[64]{0:T(512)(128)(4,1)S(1)} %get-tuple-element.269) | copy-start | bytes 196
  10.4 11.3 %copy-start.37 = (pred[64]{0:T(512)(128)(4,1)}, pred[64]{0:T(512)(128)(4,1)S(1)}, u32[]{:S(2)}) copy-start(pred[64]{0:T(512)(128)(4,1)S(1)} %get-tuple-element.270) | copy-start | bytes 196
  10.5 11.3 %copy-start.39 = (pred[64]{0:T(512)(128)(4,1)}, pred[64]{0:T(512)(128)(4,1)S(1)}, u32[]{:S(2)}) copy-start(pred[64]{0:T(512)(128)(4,1)S(1)} %get-tuple-element.271) | copy-start | bytes 196
  10.5 11.3 %copy-start.41 = (pred[64]{0:T(512)(128)(4,1)}, pred[64]{0:T(512)(128)(4,1)S(1)}, u32[]{:S(2)}) copy-start(pred[64]{0:T(512)(128)(4,1)S(1)} %get-tuple-element.272) | copy-start | bytes 196
  10.5 11.3 %copy-start.43 = (pred[64]{0:T(512)(128)(4,1)}, pred[64]{0:T(512)(128)(4,1)S(1)}, u32[]{:S(2)}) copy-start(pred[64]{0:T(512)(128)(4,1)S(1)} %get-tuple-element.273) | copy-start | bytes 196
  10.5 11.3 %copy-start.45 = (pred[64]{0:T(512)(128)(4,1)}, pred[64]{0:T(512)(128)(4,1)S(1)}, u32[]{:S(2)}) copy-start(pred[64]{0:T(512)(128)(4,1)S(1)} %get-tuple-element.274) | copy-start | bytes 196
  18.9 10.0 %copy-start.18 = (f32[2,32]{1,0:T(2,128)S(1)}, f32[2,32]{1,0:T(2,128)}, u32[]{:S(2)}) copy-start(f32[2,32]{1,0:T(2,128)} %param.34) | copy-start | bytes 772
  44.3 98.3 %copy-start.4 = (f32[2,2048]{1,0:T(2,128)S(1)}, f32[2,2048]{1,0:T(2,128)}, u32[]{:S(2)}) copy-start(f32[2,2048]{1,0:T(2,128)} %param.35) | copy-start | bytes 49156
  54.2 116.9 %copy-start.2 = (bf16[2,64,1024]{2,1,0:T(8,128)(2,1)S(1)}, bf16[2,64,1024]{2,1,0:T(8,128)(2,1)}, u32[]{:S(2)}) copy-start(bf16[2,64,1024]{2,1,0:T(8,128)(2,1)} %param.29) | copy-start | bytes 786436
  152.4 77.4 %all-gather.11.cloned.1.call-start = ((), (), s32[]{:S(2)}) async-start(), calls=%async_computation.4 | async-start | bytes 4456448 | tf_op jit(solution)/shard_map/all_gather | solution.py:211
  234.9 66.5 %copy-start.48 = (s32[64]{0:T(128)S(1)}, s32[64]{0:T(128)}, u32[]{:S(2)}) copy-start(s32[64]{0:T(128)} %param.45) | copy-start | bytes 772
  234.9 67.3 %all-to-all-start = ((bf16[2,16,2,32,1024]{4,3,1,0,2:T(8,128)(2,1)}), bf16[2,16,2,32,1024]{4,3,1,0,2:T(8,128)(2,1)}, u32[]{:S(2)}, u32[]{:S(2)}) async-start(bf16[2,16,2,32,1024]{4,3,1,0,2:T(8,128)(2,1)} %copy.110), calls=%async_computation.1 | async-start | bytes 8388608 | tf_op jit(solution)/shard_map/all_to_all | solution.py:215
  318.6 68.2 %copy-start.1 = (f32[2,2048]{1,0:T(2,128)S(1)}, f32[2,2048]{1,0:T(2,128)}, u32[]{:S(2)}) copy-start(f32[2,2048]{1,0:T(2,128)} %param.36) | copy-start | bytes 49156
  (32 other events, 144.5 us)
Sparse Core Ops, SparseCore 0:
  9.5 133.0 all-gather.8
  152.6 18.4 reduce-scatter.1
  179.3 50.5 all-gather.10
where the time goes:
time: 394 us; the launch traced here: 393 us
  waiting for transfers between devices  158 us (40%)
  blocking collectives  124 us (31%)
  matrix products  42 us (11%)
  local copies, waits for them, and re-layouts  35 us (9%)
  between operations  14.7 us (4%)
  other arithmetic  13.1 us (3%)
  starting transfers between devices  5.84 us (1%)
    all_gather x1, waiting for transfers between devices, local(): lax.all_gather(out_weight, 'req', axis=2, tiled=True)  88.4 us
    unnamed x1, blocking collectives  59.2 us
    all_gather x3, blocking collectives, merged_2(): gathered = jax.tree.map(lambda a: lax.all_gather(a, axis), part)  54.1 us
    all_gather x1, waiting for transfers between devices, local(): lax.all_gather(final_rows, 'req', axis=1, tiled=True)  50.7 us
    reduce_scatter x1, waiting for transfers between devices, local(): lax.psum_scatter(partial_out, 'tp', scatter_dimension=2, tiled=True)  18.6 us
    dot_general x1, matrix products, head_scores(): jnp.einsum('mnd,mvd->mnv', rows_hidden, head_weight, preferred_element_ty...  11.1 us
    dot_general x2, matrix products, mixer_block(): readings = jnp.einsum('tn,rcn->trc', readout, initial, precision=PRECISE)  10.1 us
    dot_general x1, matrix products, local(): jnp.einsum('mtc,mcd->mtd', normed, lax.all_gather(out_weight, 'req', axis...  9.84 us
  transfers between devices with their start and end apart: 4, of which 3 were waited for; matrix products, arithmetic and copies ran while one was open for 11% of the time, Pallas kernels for 0%

commit v1 on v0

--- a/solution.py
+++ b/solution.py
@@ -1,21 +1,17 @@
+import functools
+
 import jax
 import jax.numpy as jnp
 from jax import lax
+from jax.experimental import pallas as pl
+from jax.experimental.pallas import tpu as pltpu
 from jax.sharding import PartitionSpec as P
 
 EPSILON = 1e-05
 PRECISE = lax.Precision.HIGHEST
-
-
-def merged_2(part, axis, combine):
-    gathered = jax.tree.map(lambda a: lax.all_gather(a, axis), part)
-
-    def take(source):
-        return jax.tree.map(lambda a: lax.dynamic_index_in_dim(a, source, 0, False), gathered)
-
-    return lax.fori_loop(
-        1, lax.axis_size(axis), lambda source, state: combine(state, take(source)), take(0)
-    )
+MESH = pl.DeviceIdType.MESH
+LANES = 128
+CORES = 2
 
 
 def request_layout(lengths, step_count):
@@ -111,25 +107,315 @@
     return output.reshape(step_count, inner_width) * jax.nn.silu(gate_rows.astype(jnp.float32))
 
 
-def head_scores(head_weight, vocab_start, piece_rows):
-    rows_hidden, rows_target = piece_rows
-    logits = jnp.einsum(
-        "mnd,mvd->mnv", rows_hidden, head_weight, preferred_element_type=jnp.float32
-    )
-    peak_logit = jnp.max(logits, axis=2)
-    spread = jnp.sum(jnp.exp(logits - peak_logit[:, :, None]), axis=2)
-    local_id = rows_target[0] - vocab_start
-    matches = jnp.arange(head_weight.shape[1], dtype=jnp.int32)[None, :] == local_id[:, None]
-    picked = jnp.sum(jnp.where(matches[None, :, :], logits, 0.0), axis=2)
-    return (peak_logit, spread, picked)
-
-
-def fold_stats(first_stats, second_stats):
-    peak_logit = jnp.maximum(first_stats[0], second_stats[0])
-    spread = first_stats[1] * jnp.exp(first_stats[0] - peak_logit) + second_stats[1] * jnp.exp(
-        second_stats[0] - peak_logit
-    )
-    return (peak_logit, spread, first_stats[2] + second_stats[2])
+def split_shards(shards):
+    chips = shards // CORES
+    inner = 1
+    while inner * inner * 4 <= chips:
+        inner *= 2
+    return chips // inner, inner
+
+
+def flipped(index, mask):
+    value, bit = index, 1
+    while bit <= mask:
+        if mask & bit:
+            value = value + bit - 2 * bit * ((index // bit) % 2)
+        bit *= 2
+    return value
+
+
+def score_kernel(
+    outer,
+    inner,
+    groups,
+    gated_ref,
+    gain_ref,
+    final_gain_ref,
+    resid_ref,
+    local_ids_ref,
+    weight_ref,
+    head_ref,
+    result_ref,
+    weight,
+    head,
+    squares,
+    normed,
+    part,
+    landed,
+    total,
+    hidden,
+    final,
+    stats,
+    stats_in,
+    weight_sem,
+    head_sem,
+    square_send,
+    square_recv,
+    normed_send,
+    normed_recv,
+    part_send,
+    part_recv,
+    hidden_send,
+    hidden_recv,
+    stats_send,
+    stats_recv,
+):
+    me = lax.axis_index("req")
+    lane = lax.axis_index("tp")
+    columns = inner * CORES
+    shards = outer * columns
+    row, column = me // columns, me % columns
+    x, core = column // CORES, column % CORES
+    models, inner_part = gain_ref.shape
+    slots = gated_ref.shape[0] // models
+    share = slots // groups
+    width = resid_ref.shape[2]
+    features = width * outer
+    line_rows = outer * share
+    pending = []
+
+    def send(source, target, send_sem, recv_sem, device):
+        copy = pltpu.make_async_remote_copy(
+            src_ref=source,
+            dst_ref=target,
+            send_sem=send_sem,
+            recv_sem=recv_sem,
+            device_id=device,
+            device_id_type=MESH,
+        )
+        copy.start()
+        pending.append(copy)
+
+    def landing(buffer, recv_sem):
+        pltpu.make_async_copy(buffer, buffer, recv_sem).wait()
+
+    barrier = pltpu.get_barrier_semaphore()
+    for step in range(1, shards):
+        pl.semaphore_signal(
+            barrier,
+            inc=1,
+            device_id=(lax.rem(me + step, shards), lane),
+            device_id_type=MESH,
+        )
+    for step in range(1, groups):
+        pl.semaphore_signal(
+            barrier,
+            inc=1,
+            device_id=(me, lax.rem(lane + step, groups)),
+            device_id_type=MESH,
+        )
+
+    if len(weight_ref.shape) == 4:
+        block = weight_ref.shape[3]
+        loads = [
+            pltpu.make_async_copy(
+                weight_ref.at[index],
+                weight.at[:, :, pl.ds(index * block, block)],
+                weight_sem.at[index],
+            )
+            for index in range(columns)
+        ]
+    else:
+        loads = [pltpu.make_async_copy(weight_ref, weight, weight_sem.at[0])]
+    for load in loads:
+        load.start()
+    head_loads = [
+        pltpu.make_async_copy(head_ref.at[model], head.at[model], head_sem.at[model])
+        for model in range(models)
+    ]
+    for load in head_loads:
+        load.start()
+
+    with jax.named_scope("gated_norm"):
+        for model in range(models):
+            rows = pl.ds(model * slots, slots)
+            values = gated_ref[rows, :]
+            own = jnp.sum(values * values, axis=1, keepdims=True)
+            squares[lane, rows, :] = jnp.broadcast_to(own, (slots, LANES))
+        pl.semaphore_wait(barrier, shards - 1 + groups - 1)
+        for step in range(1, groups):
+            send(
+                squares.at[lane],
+                squares.at[lane],
+                square_send.at[step],
+                square_recv.at[lane],
+                (me, lax.rem(lane + step, groups)),
+            )
+        for step in range(1, groups):
+            other = lax.rem(lane + step, groups)
+            landing(squares.at[other], square_recv.at[other])
+        for model in range(models):
+            rows = pl.ds(model * slots, slots)
+            level = squares[0, rows, 0:1]
+            for group in range(1, groups):
+                level = level + squares[group, rows, 0:1]
+            scale = lax.rsqrt(level / (inner_part * groups) + EPSILON)
+            normed[row, rows, :] = (
+                gated_ref[rows, :] * scale * gain_ref[model : model + 1, :]
+            ).astype(jnp.bfloat16)
+
+    with jax.named_scope("out_projection"):
+        for mask in range(1, outer):
+            send(
+                normed.at[row],
+                normed.at[row],
+                normed_send.at[mask],
+                normed_recv.at[row],
+                (flipped(row, mask) * columns + column, lane),
+            )
+        for load in loads:
+            load.wait()
+        for mask in range(outer):
+            line = flipped(row, mask)
+            if mask:
+                landing(normed.at[line], normed_recv.at[line])
+            for model in range(models):
+                rows = pl.ds(model * slots, slots)
+                product = jnp.dot(
+                    normed[line, rows, :], weight[model], preferred_element_type=jnp.float32
+                ) + resid_ref[line, rows, :].astype(jnp.float32)
+                for group in range(groups):
+                    part[group, line, pl.ds(model * share, share), :] = product[
+                        group * share : (group + 1) * share
+                    ]
+            for step in range(1, groups):
+                other = lax.rem(lane + step, groups)
+                send(
+                    part.at[other, line],
+                    landed.at[lane, line],
+                    part_send.at[step, mask],
+                    part_recv.at[lane, line],
+                    (me, other),
+                )
+        for mask in range(outer):
+            line = flipped(row, mask)
+            summed = part[lane, line]
+            for step in range(1, groups):
+                other = lax.rem(lane + step, groups)
+                landing(landed.at[other, line], part_recv.at[other, line])
+                summed = summed + landed[other, line]
+            for model in range(models):
+                start = pl.multiple_of(model * line_rows + line * share, share)
+                total[pl.ds(start, share), :] = summed[model * share : (model + 1) * share]
+        hidden[row, column] = total[...].astype(jnp.bfloat16)
+
+    def normalize(source):
+        level = None
+        for line in range(outer):
+            values = hidden[line, source].astype(jnp.float32)
+            own = jnp.sum(values * values, axis=1, keepdims=True)
+            level = own if level is None else level + own
+        scale = lax.rsqrt(level / features + EPSILON)
+        start = pl.multiple_of(source * line_rows, line_rows)
+        for line in range(outer):
+            for model in range(models):
+                rows = slice(model * line_rows, (model + 1) * line_rows)
+                values = hidden[line, source, rows, :].astype(jnp.float32)
+                spot = slice(line * width, (line + 1) * width)
+                final[model, pl.ds(start, line_rows), spot] = (
+                    values * scale[rows] * final_gain_ref[model : model + 1, spot]
+                ).astype(jnp.bfloat16)
+
+    with jax.named_scope("gather_features"):
+        counter = iter(range(hidden_send.shape[0]))
+
+        def pass_on(line, source, device):
+            send(
+                hidden.at[line, source],
+                hidden.at[line, source],
+                hidden_send.at[next(counter)],
+                hidden_recv.at[line, source],
+                (device, lane),
+            )
+
+        for mask in range(1, outer):
+            pass_on(row, column, flipped(row, mask) * columns + column)
+        sibling = 1 - core
+        for mask in range(outer):
+            line = flipped(row, mask)
+            if mask:
+                landing(hidden.at[line, column], hidden_recv.at[line, column])
+            for side in range(1, inner):
+                pass_on(line, column, row * columns + flipped(x, side) * CORES + core)
+            pass_on(line, column, row * columns + x * CORES + sibling)
+        normalize(column)
+        for side in range(1, inner):
+            source = flipped(x, side) * CORES + core
+            for mask in range(outer):
+                line = flipped(row, mask)
+                landing(hidden.at[line, source], hidden_recv.at[line, source])
+                pass_on(line, source, row * columns + x * CORES + sibling)
+            normalize(source)
+        for side in range(inner):
+            source = flipped(x, side) * CORES + sibling
+            for mask in range(outer):
+                line = flipped(row, mask)
+                landing(hidden.at[line, source], hidden_recv.at[line, source])
+            normalize(source)
+
+    with jax.named_scope("head"):
+        entries = head_ref.shape[1]
+        tile = max(size for size in range(16, 401, 16) if entries % size == 0)
+        tokens = final.shape[1]
+        stats[...] = jnp.zeros_like(stats)
+        for model in range(models):
+            head_loads[model].wait()
+
+            def scan(index, state, model=model):
+                peak, spread, picked = state
+                start = pl.multiple_of(index * tile, tile)
+                logits = lax.dot_general(
+                    head[model, pl.ds(start, tile), :],
+                    final[model],
+                    (((1,), (1,)), ((), ())),
+                    preferred_element_type=jnp.float32,
+                )
+                new_peak = jnp.maximum(peak, jnp.max(logits, axis=0, keepdims=True))
+                spread = spread * jnp.exp(peak - new_peak) + jnp.sum(
+                    jnp.exp(logits - new_peak), axis=0, keepdims=True
+                )
+                entry = lax.broadcasted_iota(jnp.int32, (tile, tokens), 0) + start
+                picked = picked + jnp.sum(
+                    jnp.where(entry == local_ids_ref[0:1, :], logits, 0.0), axis=0, keepdims=True
+                )
+                return new_peak, spread, picked
+
+            zero = jnp.zeros((1, tokens), jnp.float32)
+            found = lax.fori_loop(0, entries // tile, scan, (zero - jnp.inf, zero, zero))
+            for kind in range(3):
+                for index in range(tokens // LANES):
+                    stats[index, pl.ds(3 * model + kind, 1), :] = found[kind][
+                        :, index * LANES : (index + 1) * LANES
+                    ]
+
+    with jax.named_scope("merge"):
+
+        def tile_of(shard):
+            return (((shard % columns) * outer + shard // columns) * share) // LANES
+
+        for step in range(1, shards):
+            other = lax.rem(me + step, shards)
+            send(
+                stats.at[tile_of(other)],
+                stats_in.at[me],
+                stats_send.at[step],
+                stats_recv.at[me],
+                (other, lane),
+            )
+        stats_in[me] = stats[tile_of(me)]
+        for step in range(1, shards):
+            other = lax.rem(me + step, shards)
+            landing(stats_in.at[other], stats_recv.at[other])
+        for model in range(models):
+            peaks = stats_in[:, 3 * model, :]
+            peak = jnp.max(peaks, axis=0, keepdims=True)
+            spread = jnp.sum(
+                stats_in[:, 3 * model + 1, :] * jnp.exp(peaks - peak), axis=0, keepdims=True
+            )
+            picked = jnp.sum(stats_in[:, 3 * model + 2, :], axis=0, keepdims=True)
+            result_ref[model : model + 1, :] = picked - (peak + jnp.log(spread))
+    for copy in pending:
+        copy.wait_send()
 
 
 def local(
@@ -159,10 +445,33 @@
     shards = lax.axis_size("req")
     lane_index = lax.axis_index("tp")
     shard_index = lax.axis_index("req")
-    models = gate_in.shape[0]
-    step_count = gate_in.shape[1]
-    row_count = step_count // groups
-    gated = jnp.stack(
+    outer, inner = split_shards(shards)
+    columns = inner * CORES
+    models, step_count, inner_part = gate_in.shape
+    share = step_count // groups
+    features = final_gain.shape[1]
+    width = features // outer
+    vocab_part = head_weight.shape[1]
+    tokens = shards * share
+    row, column = shard_index // columns, shard_index % columns
+    lines = [[z * columns + c for z in range(outer)] for c in range(columns)]
+    planes = [[z * columns + c for c in range(columns)] for z in range(outer)]
+
+    if out_weight.shape[2] % LANES == 0:
+        weights = lax.all_gather(out_weight, "req", axis_index_groups=planes)
+    else:
+        weights = lax.all_gather(out_weight, "req", axis=2, tiled=True, axis_index_groups=planes)
+    resid_line = lax.all_gather(resid_in, "req", axis_index_groups=lines)
+    per_group = outer // groups
+    resid_part = lax.dynamic_slice_in_dim(resid_line, (row % per_group) * width, width, 3)
+    resid_part = jnp.where(row // per_group == lane_index, resid_part, 0).reshape(
+        outer, models * step_count, width
+    )
+    every_target = lax.all_gather(targets, "req").reshape(outer, columns, groups, share)
+    own_targets = lax.dynamic_index_in_dim(every_target, lane_index, 2, False)
+    local_ids = jnp.swapaxes(own_targets, 0, 1).reshape(1, tokens) - shard_index * vocab_part
+
+    gated = jnp.concatenate(
         [
             mixer_block(
                 gate_in[model_index],
@@ -183,50 +492,50 @@
             for model_index in range(models)
         ]
     )
-    squares = lax.psum(jnp.sum(gated * gated, axis=2), "tp")
-    inner_width = gated.shape[2] * groups
-    normed = (
-        gated * lax.rsqrt(squares / inner_width + EPSILON)[:, :, None] * norm_gain[:, None, :]
-    ).astype(jnp.bfloat16)
-    partial_out = jnp.einsum(
-        "mtc,mcd->mtd",
-        normed,
-        lax.all_gather(out_weight, "req", axis=2, tiled=True),
-        preferred_element_type=jnp.float32,
-    )
-    update = lax.psum_scatter(partial_out, "tp", scatter_dimension=2, tiled=True)
-    hidden = (resid_in.astype(jnp.float32) + update).astype(jnp.bfloat16)
-    part_width = hidden.shape[2]
-    full_width = part_width * groups
-    vocab_part = head_weight.shape[1]
-    hidden_float = hidden.astype(jnp.float32)
-    final_squares = lax.psum(jnp.sum(hidden_float * hidden_float, axis=2), "tp")
-    gain_part = lax.dynamic_slice_in_dim(final_gain, lane_index * part_width, part_width, 1)
-    final_rows = (
-        hidden_float
-        * lax.rsqrt(final_squares / full_width + EPSILON)[:, :, None]
-        * gain_part[:, None, :]
-    ).astype(jnp.bfloat16)
-    every_rows, every_target = (
-        lax.all_gather(final_rows, "req", axis=1, tiled=True),
-        lax.all_gather(targets, "req", axis=0, tiled=True),
-    )
-    blocks = every_rows.reshape(models, shards, groups, row_count, part_width)
-    regrouped = lax.all_to_all(blocks, "tp", split_axis=2, concat_axis=4, tiled=True).reshape(
-        models, shards * row_count, full_width
-    )
-    target_rows = lax.dynamic_slice_in_dim(
-        every_target.reshape(shards, groups, row_count), lane_index, 1, 1
-    ).reshape(1, shards * row_count)
-    statistics = head_scores(head_weight, shard_index * vocab_part, (regrouped, target_rows))
-    merged = merged_2(statistics, "req", fold_stats)
-    peak_logit = lax.dynamic_slice_in_dim(merged[0], shard_index * row_count, row_count, 1)
-    spread = lax.dynamic_slice_in_dim(merged[1], shard_index * row_count, row_count, 1)
-    picked = lax.dynamic_slice_in_dim(merged[2], shard_index * row_count, row_count, 1)
-    scored_rows = lax.dynamic_slice_in_dim(score_flag, lane_index * row_count, row_count, 0).astype(
-        jnp.float32
-    )
-    return (picked - (peak_logit + jnp.log(spread))) * scored_rows[None, :]
+    rows = models * step_count
+    line_rows = outer * share
+    sends = outer - 1 + outer * (inner - 1) + outer * inner
+    dma = pltpu.SemaphoreType.DMA
+    vmem = pl.BlockSpec(memory_space=pltpu.VMEM)
+    anywhere = pl.BlockSpec(memory_space=pl.ANY)
+    scores = pl.pallas_call(
+        functools.partial(score_kernel, outer, inner, groups),
+        out_shape=jax.ShapeDtypeStruct((models, LANES), jnp.float32),
+        in_specs=[vmem] * 5 + [anywhere] * 2,
+        out_specs=vmem,
+        scratch_shapes=[
+            pltpu.VMEM((models, inner_part, width), jnp.bfloat16),
+            pltpu.VMEM((models, vocab_part, features), jnp.bfloat16),
+            pltpu.VMEM((groups, rows, LANES), jnp.float32),
+            pltpu.VMEM((outer, rows, inner_part), jnp.bfloat16),
+            pltpu.VMEM((groups, outer, models * share, width), jnp.float32),
+            pltpu.VMEM((groups, outer, models * share, width), jnp.float32),
+            pltpu.VMEM((models * line_rows, width), jnp.float32),
+            pltpu.VMEM((outer, columns, models * line_rows, width), jnp.bfloat16),
+            pltpu.VMEM((models, tokens, features), jnp.bfloat16),
+            pltpu.VMEM((tokens // LANES, 8, LANES), jnp.float32),
+            pltpu.VMEM((shards, 8, LANES), jnp.float32),
+            dma((columns,)),
+            dma((models,)),
+            dma((groups,)),
+            dma((groups,)),
+            dma((outer,)),
+            dma((outer,)),
+            dma((groups, outer)),
+            dma((groups, outer)),
+            dma((sends,)),
+            dma((outer, columns)),
+            dma((shards,)),
+            dma((shards,)),
+        ],
+        compiler_params=pltpu.CompilerParams(
+            collective_id=0, has_side_effects=True, vmem_limit_bytes=50 * 1024 * 1024
+        ),
+    )(gated, norm_gain, final_gain, resid_part, local_ids, weights, head_weight)
+    spot = ((column * outer + row) * share) % LANES
+    own_scores = lax.dynamic_slice_in_dim(scores, spot, share, 1)
+    scored_rows = lax.dynamic_slice_in_dim(score_flag, lane_index * share, share, 0)
+    return own_scores * scored_rows.astype(jnp.float32)[None, :]
 
 
 def solution(mesh):

time: 394 us -> 229 us (0.58)
  waiting for transfers between devices: 158 us -> 1.45 us
  Pallas kernels: 0 us -> 107 us
  blocking collectives: 124 us -> 63.4 us
  local copies, waits for them, and re-layouts: 35 us -> 11.7 us
  matrix products: 42 us -> 21.6 us
  starting transfers between devices: 5.84 us -> 0.04 us
  other arithmetic: 13.1 us -> 7.69 us
    all_gather x2, waiting for transfers between devices: 139 us -> 0.04 us  [the longest x1 0.02 us: local(): resid_line = lax.all_gather(resid_in, 'req', axis_index_groups=lines)]
    pallas_call x0 -> x1, Pallas kernels: none -> 107 us  [local(): pl.pallas_call(functools.partial(score_kernel, outer, inner, groups), out...]
    all_gather x3 -> x0, blocking collectives: 54.1 us -> none  [merged_2(): gathered = jax.tree.map(lambda a: lax.all_gather(a, axis), part)]
    dot_general x2 -> x0, matrix products: 20.9 us -> none  [the longest x1 11.1 us: head_scores(): jnp.einsum('mnd,mvd->mnv', rows_hidden, head_weight, preferred_element_ty...]
    reduce_scatter x1 -> x0, waiting for transfers between devices: 18.6 us -> none  [local(): lax.psum_scatter(partial_out, 'tp', scatter_dimension=2, tiled=True)]
    reshape x3 -> x1, local copies, waits for them, and re-layouts: 12.9 us -> 0.08 us  [local(): lax.all_gather(targets, 'req').reshape(outer, columns, groups, share)]
    psum x2 -> x0, blocking collectives: 10.8 us -> none  [the longest x1 5.84 us: local(): squares = lax.psum(jnp.sum(gated * gated, axis=2), 'tp')]
    all_to_all x1 -> x0, local copies, waits for them, and re-layouts: 8.61 us -> none  [local(): lax.all_to_all(blocks, 'tp', split_axis=2, concat_axis=4, tiled=True)]
  transfers between devices with their start and end apart: 4 -> 2, of which waited for: 3 -> 0; matrix products, arithmetic and copies ran while one was open for 11% -> 18% of each run, Pallas kernels for 0% -> 0%
where the time goes in v1:
time: 229 us; the launch traced here: 228 us
  Pallas kernels  107 us (47%)
  blocking collectives  63.4 us (28%)
  matrix products  21.6 us (9%)
  between operations  15.2 us (7%)
  local copies, waits for them, and re-layouts  11.7 us (5%)
  other arithmetic  7.69 us (3%)
    pallas_call x1, Pallas kernels, local(): pl.pallas_call(functools.partial(score_kernel, outer, inner, groups), out...  107 us
    unnamed x1, blocking collectives  63.4 us
    dot_general x2, matrix products, mixer_block(): readings = jnp.einsum('tn,rcn->trc', readout, initial, precision=PRECISE)  10 us
    dot_general x12, matrix products, causal_conv(): jnp.dot(member_bf, history[:, slot_index, :], preferred_element_type=jnp....  5.96 us
    dot_general x2, matrix products, mixer_block(): jnp.einsum('tsh,shp->thp', kernel_full, step_size[:, :, None] * values, p...  4.74 us
  transfers between devices with their start and end apart: 2, of which 0 were waited for; matrix products, arithmetic and copies ran while one was open for 18% of the time, Pallas kernels for 0%

profile of v1, /device:TPU:0, one launch (start us, length us, event | category | flops | bytes accessed | tf_op | source)
XLA Modules:
  0.0 228.3 jit_solution(3777985017321476777)
XLA Ops:
  6.5 0.7 all-gather.6.cloned.1.call-update
  7.3 0.7 all-gather.8.cloned.1.call-update
  8.0 0.8 reduce-window.4
  8.8 0.7 compare_and_fusion
  9.5 0.7 fusion.143
  10.2 1.1 slice_convert_fusion.1
  11.3 0.9 slice_bitcast_fusion
  12.2 0.9 slice_bitcast_fusion.1
  13.1 0.9 slice_bitcast_fusion.2
  14.5 0.7 fusion.153
  16.0 0.7 fusion.152
  18.4 1.0 divide_multiply_fusion
  20.3 4.9 %fusion.10 = f32[64,2048]{1,0:T(8,128)S(1)} fusion(bf16[2,3,2048,128]{3,2,1,0:T(8,128)(2,1)} %param.39, f32[3]{0:T(128)S(1)} %get-tuple-element.61, f32[64,3]{0,1:T(4,128)S(1)} %fusion.123, f32[64,256]{1,0:T(8,128)S(1)} %divide_multiply_fusion.2), kind=kOutput, calls=%fused_computation.14 | convolution fusion | flops 606208000 | bytes 2132480 | tf_op jit(solution)/shard_map/tn,rcn->trc/dot_general | solution.py:102
  28.2 2.1 fusion.13
  30.3 1.1 copy.110
  32.1 2.5 %divide_multiply_fusion.1 = f32[64,2048]{1,0:T(8,128)S(1)} fusion(f32[64,2048]{1,0:T(8,128)S(1)} %fusion.86, f32[64,2048]{1,0:T(8,128)S(1)} %fusion.89, f32[61,2048]{1,0:T(8,128)} %get-tuple-element.82, f32[62,2048]{1,0:T(8,128)} %get-tuple-element.84, f32[63,2048]{1,0:T(8,128)} %get-tuple-element.86, f32[2048]{0:T(1024)} %bitcast.235, f32[2048]{0:T(1024)} %bitcast.236, ...), kind=kOutput, calls=%fused_computation.78 | convolution fusion | flops 4718784 | bytes 3404800 | tf_op jit(solution)/shard_map/dot_general | solution.py:32
  35.9 5.1 %fusion.11 = f32[64,2048]{1,0:T(8,128)S(1)} fusion(f32[3]{0:T(128)S(1)} %copy-done.52, bf16[2,3,2048,128]{3,2,1,0:T(8,128)(2,1)} %param.39, f32[64,3]{0,1:T(4,128)S(1)} %copy-done.13, f32[64,256]{1,0:T(8,128)S(1)} %divide_multiply_fusion.3), kind=kOutput, calls=%fused_computation.15 | convolution fusion | flops 606208000 | bytes 2132480 | tf_op jit(solution)/shard_map/tn,rcn->trc/dot_general | solution.py:102
  41.4 0.7 gather_fusion
  42.6 2.7 %fusion.15 = f32[64,32,64]{0,2,1:T(8,128)S(1)} fusion(f32[64,32,64]{0,2,1:T(8,128)S(1)} %bitcast.226, f32[64,32,64]{0,2,1:T(8,128)S(1)} %bitcast.229, f32[32]{0:T(128)} %get-tuple-element.55, f32[64,32]{0,1:T(8,128)S(1)} %fusion.19, f32[64,64]{1,0:T(8,128)S(1)} %fusion.67, f32[64,32]{0,1:T(8,128)S(1)} %copy.89, f32[64,32]{0,1:T(8,128)S(1)} %get-tuple-element.30, ...), kind=kOutput, calls=%fused_computation.21 | convolution fusion | flops 101842944 | bytes 1618048 | tf_op jit(solution)/shard_map/tsh,shp->thp/dot_general | solution.py:94
  47.3 63.4 %all-reduce.13 = s32[4,4,2,32]{3,2,1,0:T(2,128)S(1)} all-reduce(s32[4,4,2,32]{3,2,1,0:T(2,128)S(1)} %reshape.326), channel_id=3, replica_groups=mesh['req'=16,'tp'=2] {'req'}, use_global_device_ids=true, to_apply=%add.12 | all-reduce | flops 1024 | bytes 8192
  110.9 1.5 fusion.35
  112.5 1.1 dynamic-slice_select_fusion
  113.7 107.1 %shard_map.199 = f32[2,128]{1,0:T(2,128)S(1)} custom-call(f32[128,2048]{1,0:T(8,128)S(1)} %pad_maximum_fusion.gated_ref, f32[2,2048]{1,0:T(2,128)S(1)} %copy-done, f32[2,2048]{1,0:T(2,128)S(1)} %copy-done.1, bf16[4,128,512]{2,1,0:T(8,128)(2,1)S(1)} %bitcast.224, s32[1,512]{1,0:T(1,128)S(1)} %sub.169.local_ids_ref, bf16[4,2,2048,128]{3,2,1,0:T(8,128)(2,1)} %bitcast.225, ...), custom_call_target="tpu_custom_call" | custom-call | tf_op jit(solution)/shard_map/pallas_call | solution.py:501
  220.8 0.6 dynamic-slice_multiply_fusion
  (171 shorter events, 10.4 us)
Async XLA Ops:
  6.5 106.0 %all-gather.6.cloned.1.call-start = ((), (), s32[]{:S(2)}) async-start(), calls=%async_computation | async-start | bytes 1310720 | tf_op jit(solution)/shard_map/all_gather | solution.py:464
  7.3 106.4 %all-gather.8.cloned.1.call-start = ((), (), s32[]{:S(2)}) async-start(), calls=%async_computation.1 | async-start | bytes 5242880 | tf_op jit(solution)/shard_map/all_gather | solution.py:461
  9.5 18.2 %copy-start.21 = (pred[3]{0:T(512)(128)(4,1)}, pred[3]{0:T(512)(128)(4,1)S(1)}, u32[]{:S(2)}) copy-start(pred[3]{0:T(512)(128)(4,1)S(1)} %get-tuple-element.6) | copy-start | bytes 13
  12.2 3.7 %copy-start.5 = (f32[2,4,2048]{2,1,0:T(4,128)S(1)}, f32[2,4,2048]{2,1,0:T(4,128)}, u32[]{:S(2)}) copy-start(f32[2,4,2048]{2,1,0:T(4,128)} %param.28) | copy-start | bytes 196612
  12.2 4.5 %copy-start.7 = (bf16[2,3,3,256]{3,0,2,1:T(2,128)(2,1)S(1)}, bf16[2,3,3,256]{3,0,2,1:T(2,128)(2,1)}, u32[]{:S(2)}) copy-start(bf16[2,3,3,256]{3,0,2,1:T(2,128)(2,1)} %param.38) | copy-start | bytes 27652
  13.1 4.7 %copy-start.9 = (f32[2,4,256]{2,1,0:T(4,128)S(1)}, f32[2,4,256]{2,1,0:T(4,128)}, u32[]{:S(2)}) copy-start(f32[2,4,256]{2,1,0:T(4,128)} %param.29) | copy-start | bytes 24580
  13.1 5.3 %copy-start.2 = (bf16[2,64,2048]{2,1,0:T(8,128)(2,1)S(1)}, bf16[2,64,2048]{2,1,0:T(8,128)(2,1)}, u32[]{:S(2)}) copy-start(bf16[2,64,2048]{2,1,0:T(8,128)(2,1)} %param.24) | copy-start | bytes 1572868
  14.3 6.0 %copy-start.51 = (f32[3]{0:T(128)}, f32[3]{0:T(128)S(1)}, u32[]{:S(2)}) copy-start(f32[3]{0:T(128)S(1)} %get-tuple-element.61) | copy-start | bytes 40
  15.9 3.5 %copy-start.23 = (pred[64]{0:T(512)(128)(4,1)}, pred[64]{0:T(512)(128)(4,1)S(1)}, u32[]{:S(2)}) copy-start(pred[64]{0:T(512)(128)(4,1)S(1)} %get-tuple-element.63) | copy-start | bytes 196
  15.9 3.5 %copy-start.25 = (pred[64]{0:T(512)(128)(4,1)}, pred[64]{0:T(512)(128)(4,1)S(1)}, u32[]{:S(2)}) copy-start(pred[64]{0:T(512)(128)(4,1)S(1)} %get-tuple-element.64) | copy-start | bytes 196
  15.9 3.5 %copy-start.27 = (pred[64]{0:T(512)(128)(4,1)}, pred[64]{0:T(512)(128)(4,1)S(1)}, u32[]{:S(2)}) copy-start(pred[64]{0:T(512)(128)(4,1)S(1)} %get-tuple-element.65) | copy-start | bytes 196
  19.8 5.8 %copy-start.19 = (f32[2,32]{1,0:T(2,128)S(1)}, f32[2,32]{1,0:T(2,128)}, u32[]{:S(2)}) copy-start(f32[2,32]{1,0:T(2,128)} %param.31) | copy-start | bytes 772
  19.8 5.7 %copy-start.20 = (f32[2,32]{1,0:T(2,128)S(1)}, f32[2,32]{1,0:T(2,128)}, u32[]{:S(2)}) copy-start(f32[2,32]{1,0:T(2,128)} %param.30) | copy-start | bytes 772
  19.8 5.8 %copy-start.6 = (bf16[2,64,32]{1,2,0:T(8,128)(2,1)S(1)}, bf16[2,64,32]{1,2,0:T(8,128)(2,1)}, u32[]{:S(2)}) copy-start(bf16[2,64,32]{1,2,0:T(8,128)(2,1)} %param.26) | copy-start | bytes 24580
  19.9 5.8 %copy-start.12 = (f32[64,3]{0,1:T(4,128)}, f32[64,3]{0,1:T(4,128)S(1)}, u32[]{:S(2)}) copy-start(f32[64,3]{0,1:T(4,128)S(1)} %fusion.123) | copy-start | bytes 2308
  19.9 7.2 %copy-start.18 = (f32[2,32]{1,0:T(2,128)S(1)}, f32[2,32]{1,0:T(2,128)}, u32[]{:S(2)}) copy-start(f32[2,32]{1,0:T(2,128)} %param.32) | copy-start | bytes 772
  32.1 3.8 %copy-start.13 = (f32[64,3]{0,1:T(4,128)S(1)}, f32[64,3]{0,1:T(4,128)}, u32[]{:S(2)}) copy-start(f32[64,3]{0,1:T(4,128)} %copy-done.12) | copy-start | bytes 2308
  32.1 3.8 %copy-start.52 = (f32[3]{0:T(128)S(1)}, f32[3]{0:T(128)}, u32[]{:S(2)}) copy-start(f32[3]{0:T(128)} %copy-done.51) | copy-start | bytes 40
  35.0 7.1 %copy-start.22 = (pred[3]{0:T(512)(128)(4,1)S(1)}, pred[3]{0:T(512)(128)(4,1)}, u32[]{:S(2)}) copy-start(pred[3]{0:T(512)(128)(4,1)} %copy-done.21) | copy-start | bytes 13
  41.0 4.7 %copy-start.50 = (u32[32]{0:T(128)S(1)}, u32[32]{0:T(128)}, u32[]{:S(2)}) copy-start(u32[32]{0:T(128)} %constant.159) | copy-start | bytes 388
  41.0 5.9 %copy-start.48 = (s32[64]{0:T(128)S(1)}, s32[64]{0:T(128)}, u32[]{:S(2)}) copy-start(s32[64]{0:T(128)} %param.42) | copy-start | bytes 772
  41.0 69.8 %copy-start.49 = (s32[64]{0:T(128)S(1)}, s32[64]{0:T(128)}, u32[]{:S(2)}) copy-start(s32[64]{0:T(128)} %param.43) | copy-start | bytes 772
  45.6 68.1 %copy-start = (f32[2,2048]{1,0:T(2,128)S(1)}, f32[2,2048]{1,0:T(2,128)}, u32[]{:S(2)}) copy-start(f32[2,2048]{1,0:T(2,128)} %gain_ref.1) | copy-start | bytes 49156
  45.6 68.1 %copy-start.1 = (f32[2,2048]{1,0:T(2,128)S(1)}, f32[2,2048]{1,0:T(2,128)}, u32[]{:S(2)}) copy-start(f32[2,2048]{1,0:T(2,128)} %final_gain_ref.1) | copy-start | bytes 49156
  (31 other events, 103.4 us)
Sparse Core Ops, SparseCore 0:
  8.9 30.7 all-gather.5
  41.2 34.3 all-gather.7

commit v2 on v1

--- a/solution.py
+++ b/solution.py
@@ -12,99 +12,174 @@
 MESH = pl.DeviceIdType.MESH
 LANES = 128
 CORES = 2
-
-
-def request_layout(lengths, step_count):
-    starts = jnp.cumsum(lengths) - lengths
-    time_index = jnp.arange(step_count, dtype=jnp.int32)
-    segment = jnp.sum((time_index[:, None] >= starts[None, 1:]).astype(jnp.int32), axis=1)
-    member = segment[:, None] == jnp.arange(lengths.shape[0], dtype=jnp.int32)[None, :]
-    first_step = jnp.sum(jnp.where(member, starts[None, :], 0), axis=1)
-    return (starts, segment, member, time_index - first_step)
-
-
-def causal_conv(stream, kernel, history, member, offset):
-    tap_count = kernel.shape[0]
-    history_len = tap_count - 1
-    current = stream.astype(jnp.float32)
-    member_bf = member.astype(jnp.bfloat16)
-    slot_values = [
-        jnp.dot(member_bf, history[:, slot_index, :], preferred_element_type=jnp.float32)
-        for slot_index in range(history_len)
-    ]
-    output = kernel[history_len][None, :] * current
-    for lag_steps in range(1, tap_count):
-        shifted = jnp.concatenate(
-            [jnp.zeros((lag_steps, current.shape[1]), current.dtype), current[:-lag_steps]], axis=0
+CHUNK = 256
+
+
+def halves(values):
+    high = values.astype(jnp.bfloat16)
+    return high, (values - high.astype(jnp.float32)).astype(jnp.bfloat16)
+
+
+def dot_f32(left, right, contract=((1,), (0,))):
+    return lax.dot_general(left, right, (contract, ((), ())), preferred_element_type=jnp.float32)
+
+
+def request_place(lengths_ref, shape, axis):
+    slot = lax.broadcasted_iota(jnp.int32, shape, axis)
+    segment, first, start = jnp.zeros_like(slot), jnp.zeros_like(slot), 0
+    for request in range(1, lengths_ref.shape[1]):
+        start = start + lengths_ref[0, request - 1]
+        later = slot >= start
+        segment = segment + later.astype(jnp.int32)
+        first = jnp.where(later, start, first)
+    return segment, slot - first
+
+
+def conv_silu(current, taps, history, requests, segment, offset):
+    tap_count = len(taps)
+    output = taps[tap_count - 1] * current
+    for lag in range(1, tap_count):
+        earlier = pltpu.roll(current, lag, 0)
+        for request in range(requests):
+            for begin in range(lag):
+                chosen = (segment == request) & (offset == begin)
+                earlier = jnp.where(chosen, history[request][begin - lag + tap_count - 1], earlier)
+        output = output + taps[tap_count - 1 - lag] * earlier
+    return jax.nn.silu(output)
+
+
+def mixer(
+    model,
+    gate_ref,
+    mix_ref,
+    keys_ref,
+    step_ref,
+    kernel_mix_ref,
+    kernel_keys_ref,
+    step_bias_ref,
+    decay_rate_ref,
+    skip_ref,
+    history_mix_ref,
+    history_keys_ref,
+    state_ref,
+    lengths_ref,
+    continued_ref,
+    gated,
+):
+    slots, inner_part = mix_ref.shape[1:]
+    heads = step_ref.shape[2]
+    head_size = inner_part // heads
+    requests, states = state_ref.shape[1], state_ref.shape[3]
+    taps = kernel_mix_ref.shape[1]
+    several = CHUNK // head_size
+
+    def rows_of(history_ref, spot):
+        return [
+            [
+                history_ref[model, pl.ds(request * (taps - 1) + slot, 1), spot]
+                for slot in range(taps - 1)
+            ]
+            for request in range(requests)
+        ]
+
+    segment, offset = request_place(lengths_ref, (slots, CHUNK), 0)
+    every = slice(None)
+    wide = keys_ref.shape[2]
+    key_segment, key_offset = request_place(lengths_ref, (slots, wide), 0)
+    projected = conv_silu(
+        keys_ref[model].astype(jnp.float32),
+        [kernel_keys_ref[model, pl.ds(tap, 1), :] for tap in range(taps)],
+        rows_of(history_keys_ref, every),
+        requests,
+        key_segment,
+        key_offset,
+    )
+    inject, readout = projected[:, :states], projected[:, states:]
+    intersection = lax.dot_general(
+        readout,
+        inject,
+        (((1,), (1,)), ((), ())),
+        precision=PRECISE,
+        preferred_element_type=jnp.float32,
+    )
+    row_segment = segment[:, :states]
+    by_request = []
+    for request in range(requests):
+        keep = continued_ref[0, request].astype(jnp.float32)
+        part = jnp.where(row_segment == request, readout, 0.0) * keep
+        by_request.append(jnp.concatenate(halves(part), axis=0))
+
+    square = (slots, slots)
+    to_segment, _ = request_place(lengths_ref, square, 0)
+    from_segment, _ = request_place(lengths_ref, square, 1)
+    to_slot = lax.broadcasted_iota(jnp.int32, square, 0)
+    from_slot = lax.broadcasted_iota(jnp.int32, square, 1)
+    causal = ((to_segment == from_segment) & (to_slot >= from_slot)).astype(jnp.float32)
+    same = (to_slot == from_slot).astype(jnp.float32)
+
+    raw = step_ref[model].astype(jnp.float32) + step_bias_ref[pl.ds(model, 1), :]
+    step_size = jnp.maximum(raw, 0.0) + jnp.log1p(jnp.exp(-jnp.abs(raw)))
+    log_decay = -step_size * decay_rate_ref[pl.ds(model, 1), :]
+    running = jnp.dot(causal, log_decay, precision=PRECISE, preferred_element_type=jnp.float32)
+    carried = jnp.exp(jnp.minimum(running, 0.0))
+    per_head = jnp.concatenate([running, step_size, carried], axis=0)
+    strength = jnp.concatenate([causal * intersection] * several, axis=1)
+    causal_wide = jnp.concatenate([causal] * several, axis=1)
+    same_wide = jnp.concatenate([same] * several, axis=1)
+    block_shape = (several * slots, CHUNK)
+    block_row = lax.broadcasted_iota(jnp.int32, block_shape, 0)
+    block_lane = lax.broadcasted_iota(jnp.int32, block_shape, 1)
+    own_block = jnp.zeros(block_shape, jnp.float32)
+    for index in range(several):
+        inside = (
+            (block_row >= index * slots)
+            & (block_row < (index + 1) * slots)
+            & (block_lane >= index * head_size)
+            & (block_lane < (index + 1) * head_size)
         )
-        earlier = jnp.zeros_like(current)
-        for slot_index in range(history_len):
-            earlier = earlier + jnp.where(
-                (offset - lag_steps == slot_index - history_len)[:, None],
-                slot_values[slot_index],
-                0.0,
-            )
-        output = output + kernel[history_len - lag_steps][None, :] * jnp.where(
-            (offset >= lag_steps)[:, None], shifted, earlier
+        own_block = jnp.where(inside, 1.0, own_block)
+
+    def chunk(index, _):
+        start = pl.multiple_of(index * CHUNK, CHUNK)
+        spot = pl.ds(start, CHUNK)
+        mixed = conv_silu(
+            mix_ref[model, :, spot].astype(jnp.float32),
+            [kernel_mix_ref[model, pl.ds(tap, 1), spot] for tap in range(taps)],
+            rows_of(history_mix_ref, spot),
+            requests,
+            segment,
+            offset,
         )
-    return jax.nn.silu(output)
-
-
-def mixer_block(
-    gate_rows,
-    mix_rows,
-    keys_rows,
-    step_raw,
-    kernel_mix,
-    kernel_keys,
-    step_bias,
-    decay_rate,
-    skip_gain,
-    history_mix,
-    history_keys,
-    start_state,
-    lengths,
-    continued,
-):
-    step_count = gate_rows.shape[0]
-    head_count = step_raw.shape[1]
-    inner_width = mix_rows.shape[1]
-    head_size = inner_width // head_count
-    states = start_state.shape[2]
-    starts, segment, member, offset = request_layout(lengths, step_count)
-    keep_state = continued.astype(jnp.bfloat16)
-    mixed = causal_conv(
-        mix_rows, kernel_mix, history_mix * keep_state[:, None, None], member, offset
-    )
-    projected = causal_conv(
-        keys_rows, kernel_keys, history_keys * keep_state[:, None, None], member, offset
-    )
-    inject = projected[:, :states]
-    readout = projected[:, states:]
-    step_size = jax.nn.softplus(step_raw.astype(jnp.float32) + step_bias[None, :])
-    log_decay = -step_size * decay_rate[None, :]
-    running = jnp.cumsum(log_decay, axis=0)
-    time_index = jnp.arange(step_count, dtype=jnp.int32)
-    causal = (segment[:, None] == segment[None, :]) & (time_index[:, None] >= time_index[None, :])
-    spread = jnp.minimum(running[:, None, :] - running[None, :, :], 0.0)
-    transfer = jnp.where(causal[:, :, None], jnp.exp(spread), 0.0)
-    intersection = jnp.dot(readout, inject.T, precision=PRECISE)
-    kernel_full = transfer * intersection[:, :, None]
-    values = mixed.reshape(step_count, head_count, head_size)
-    output = jnp.einsum(
-        "tsh,shp->thp", kernel_full, step_size[:, :, None] * values, precision=PRECISE
-    )
-    before = jnp.take(running - log_decay, starts, axis=0)
-    member_float = member.astype(jnp.float32)
-    entry_level = jnp.dot(member_float, before, precision=PRECISE)
-    carried = jnp.exp(jnp.minimum(running - entry_level, 0.0))
-    initial = start_state.astype(jnp.float32) * keep_state.astype(jnp.float32)[:, None, None]
-    readings = jnp.einsum("tn,rcn->trc", readout, initial, precision=PRECISE)
-    chosen = jnp.sum(member_float[:, :, None] * readings, axis=1).reshape(
-        step_count, head_count, head_size
-    )
-    output = output + carried[:, :, None] * chosen + skip_gain[None, :, None] * values
-    return output.reshape(step_count, inner_width) * jax.nn.silu(gate_rows.astype(jnp.float32))
+        first_unit = lax.broadcasted_iota(jnp.int32, (heads, CHUNK), 0) * head_size
+        unit = lax.broadcasted_iota(jnp.int32, (heads, CHUNK), 1) + start
+        of_head = ((unit >= first_unit) & (unit < first_unit + head_size)).astype(jnp.float32)
+        spread_out = jnp.dot(
+            per_head, of_head, precision=PRECISE, preferred_element_type=jnp.float32
+        )
+        run_to = spread_out[:slots]
+        step_wide = spread_out[slots : 2 * slots]
+        carried_wide = spread_out[2 * slots :]
+        run_from = jnp.sum(run_to * same_wide, axis=0, keepdims=True)
+        decay = jnp.exp(jnp.minimum(run_to - run_from, 0.0) * causal_wide)
+        attend_high, attend_low = halves(decay * strength)
+        values = jnp.concatenate([step_wide * mixed] * several, axis=0) * own_block
+        value_high, value_low = halves(values)
+        output = (
+            dot_f32(attend_high, value_high)
+            + dot_f32(attend_high, value_low)
+            + dot_f32(attend_low, value_high)
+        )
+        readings = None
+        for request in range(requests):
+            term = dot_f32(by_request[request], state_ref[model, request, spot, :], ((1,), (1,)))
+            readings = term if readings is None else readings + term
+        chosen = readings[:slots] + readings[slots:]
+        output = output + carried_wide * chosen + skip_ref[pl.ds(model, 1), spot] * mixed
+        gate = gate_ref[model, :, spot].astype(jnp.float32)
+        gated[pl.ds(model * slots, slots), spot] = output * jax.nn.silu(gate)
+        return 0
+
+    lax.fori_loop(0, inner_part // CHUNK, chunk, 0)
 
 
 def split_shards(shards):
@@ -128,14 +203,31 @@
     outer,
     inner,
     groups,
-    gated_ref,
+    gate_ref,
+    mix_ref,
+    keys_ref,
+    step_ref,
+    kernel_mix_ref,
+    kernel_keys_ref,
+    step_bias_ref,
+    decay_rate_ref,
+    skip_ref,
+    history_mix_ref,
+    history_keys_ref,
     gain_ref,
     final_gain_ref,
     resid_ref,
-    local_ids_ref,
+    target_ref,
+    lengths_ref,
+    continued_ref,
+    state_ref,
     weight_ref,
     head_ref,
     result_ref,
+    state,
+    gated_ref,
+    resid,
+    targets_in,
     weight,
     head,
     squares,
@@ -147,7 +239,14 @@
     final,
     stats,
     stats_in,
+    state_sem,
+    resid_send,
+    resid_recv,
+    target_send,
+    target_recv,
     weight_sem,
+    weight_send,
+    weight_recv,
     head_sem,
     square_send,
     square_recv,
@@ -167,9 +266,11 @@
     row, column = me // columns, me % columns
     x, core = column // CORES, column % CORES
     models, inner_part = gain_ref.shape
-    slots = gated_ref.shape[0] // models
+    slots = gate_ref.shape[1]
     share = slots // groups
-    width = resid_ref.shape[2]
+    width = resid.shape[3]
+    per_group = outer // groups
+    sibling = 1 - core
     features = width * outer
     line_rows = outer * share
     pending = []
@@ -205,20 +306,18 @@
             device_id_type=MESH,
         )
 
-    if len(weight_ref.shape) == 4:
-        block = weight_ref.shape[3]
-        loads = [
-            pltpu.make_async_copy(
-                weight_ref.at[index],
-                weight.at[:, :, pl.ds(index * block, block)],
-                weight_sem.at[index],
-            )
-            for index in range(columns)
-        ]
-    else:
-        loads = [pltpu.make_async_copy(weight_ref, weight, weight_sem.at[0])]
-    for load in loads:
-        load.start()
+    state_load = pltpu.make_async_copy(state_ref, state, state_sem)
+    state_load.start()
+    block = weight_ref.shape[2]
+    exchanged = block % LANES == 0
+
+    def columns_of(source):
+        return weight.at[:, :, pl.ds(pl.multiple_of(source * block, block), block)]
+
+    weight_load = pltpu.make_async_copy(
+        weight_ref, columns_of(column) if exchanged else weight, weight_sem
+    )
+    weight_load.start()
     head_loads = [
         pltpu.make_async_copy(head_ref.at[model], head.at[model], head_sem.at[model])
         for model in range(models)
@@ -226,13 +325,75 @@
     for load in head_loads:
         load.start()
 
+    pl.semaphore_wait(barrier, shards - 1 + groups - 1)
+
+    def resid_copy(index):
+        return pltpu.make_async_remote_copy(
+            src_ref=resid_ref.at[:, :, pl.ds(index * width, width)],
+            dst_ref=resid.at[row],
+            send_sem=resid_send.at[index],
+            recv_sem=resid_recv.at[row],
+            device_id=((lane * per_group + index) * columns + column, lane),
+            device_id_type=MESH,
+        )
+
+    with jax.named_scope("early_sends"):
+        if exchanged:
+            for side in range(1, inner):
+                send(
+                    weight_ref,
+                    columns_of(column),
+                    weight_send.at[side],
+                    weight_recv.at[column],
+                    (row * columns + flipped(x, side) * CORES + core, lane),
+                )
+            send(
+                weight_ref,
+                columns_of(column),
+                weight_send.at[0],
+                weight_recv.at[column],
+                (row * columns + x * CORES + sibling, lane),
+            )
+        for index in range(per_group):
+            pl.when(lane * per_group + index != row)(lambda index=index: resid_copy(index).start())
+        for step in range(1, shards):
+            send(
+                target_ref,
+                targets_in.at[me],
+                target_send.at[step],
+                target_recv.at[me],
+                (lax.rem(me + step, shards), lane),
+            )
+        targets_in[me] = target_ref[...]
+
+    with jax.named_scope("mixer"):
+        state_load.wait()
+        for model in range(models):
+            mixer(
+                model,
+                gate_ref,
+                mix_ref,
+                keys_ref,
+                step_ref,
+                kernel_mix_ref,
+                kernel_keys_ref,
+                step_bias_ref,
+                decay_rate_ref,
+                skip_ref,
+                history_mix_ref,
+                history_keys_ref,
+                state,
+                lengths_ref,
+                continued_ref,
+                gated_ref,
+            )
+
     with jax.named_scope("gated_norm"):
         for model in range(models):
             rows = pl.ds(model * slots, slots)
             values = gated_ref[rows, :]
             own = jnp.sum(values * values, axis=1, keepdims=True)
             squares[lane, rows, :] = jnp.broadcast_to(own, (slots, LANES))
-        pl.semaphore_wait(barrier, shards - 1 + groups - 1)
         for step in range(1, groups):
             send(
                 squares.at[lane],
@@ -263,8 +424,39 @@
                 normed_recv.at[row],
                 (flipped(row, mask) * columns + column, lane),
             )
-        for load in loads:
-            load.wait()
+        weight_load.wait()
+        if exchanged:
+            for side in range(1, inner):
+                other = flipped(x, side) * CORES + core
+                landing(columns_of(other), weight_recv.at[other])
+                send(
+                    columns_of(other),
+                    columns_of(other),
+                    weight_send.at[inner + side - 1],
+                    weight_recv.at[other],
+                    (row * columns + x * CORES + sibling, lane),
+                )
+
+        @pl.when(row // per_group == lane)
+        def _():
+            for index in range(per_group):
+
+                @pl.when(lane * per_group + index == row)
+                def _():
+                    resid[row] = resid_ref[:, :, index * width : (index + 1) * width]
+
+            for mask in range(1, outer):
+                line = flipped(row, mask)
+                landing(resid.at[line], resid_recv.at[line])
+
+        @pl.when(row // per_group != lane)
+        def _():
+            resid[...] = jnp.zeros_like(resid)
+
+        if exchanged:
+            for side in range(inner):
+                other = flipped(x, side) * CORES + sibling
+                landing(columns_of(other), weight_recv.at[other])
         for mask in range(outer):
             line = flipped(row, mask)
             if mask:
@@ -273,7 +465,7 @@
                 rows = pl.ds(model * slots, slots)
                 product = jnp.dot(
                     normed[line, rows, :], weight[model], preferred_element_type=jnp.float32
-                ) + resid_ref[line, rows, :].astype(jnp.float32)
+                ) + resid[line, model].astype(jnp.float32)
                 for group in range(groups):
                     part[group, line, pl.ds(model * share, share), :] = product[
                         group * share : (group + 1) * share
@@ -330,7 +522,6 @@
 
         for mask in range(1, outer):
             pass_on(row, column, flipped(row, mask) * columns + column)
-        sibling = 1 - core
         for mask in range(outer):
             line = flipped(row, mask)
             if mask:
@@ -358,6 +549,16 @@
         tile = max(size for size in range(16, 401, 16) if entries % size == 0)
         tokens = final.shape[1]
         stats[...] = jnp.zeros_like(stats)
+        for step in range(1, shards):
+            other = lax.rem(me + step, shards)
+            landing(targets_in.at[other], target_recv.at[other])
+        tiles = [None] * (tokens // LANES)
+        for source in range(columns):
+            for line in range(outer):
+                index = ((source * outer + line) * share) // LANES
+                term = targets_in[line * columns + source, 0:1, :]
+                tiles[index] = term if tiles[index] is None else tiles[index] + term
+        local_ids = jnp.concatenate(tiles, axis=1) - me * entries
         for model in range(models):
             head_loads[model].wait()
 
@@ -376,7 +577,7 @@
                 )
                 entry = lax.broadcasted_iota(jnp.int32, (tile, tokens), 0) + start
                 picked = picked + jnp.sum(
-                    jnp.where(entry == local_ids_ref[0:1, :], logits, 0.0), axis=0, keepdims=True
+                    jnp.where(entry == local_ids, logits, 0.0), axis=0, keepdims=True
                 )
                 return new_peak, spread, picked
 
@@ -414,6 +615,8 @@
             )
             picked = jnp.sum(stats_in[:, 3 * model + 2, :], axis=0, keepdims=True)
             result_ref[model : model + 1, :] = picked - (peak + jnp.log(spread))
+    for index in range(per_group):
+        pl.when(lane * per_group + index != row)(lambda index=index: resid_copy(index).wait_send())
     for copy in pending:
         copy.wait_send()
 
@@ -454,56 +657,39 @@
     vocab_part = head_weight.shape[1]
     tokens = shards * share
     row, column = shard_index // columns, shard_index % columns
-    lines = [[z * columns + c for z in range(outer)] for c in range(columns)]
-    planes = [[z * columns + c for c in range(columns)] for z in range(outer)]
-
-    if out_weight.shape[2] % LANES == 0:
-        weights = lax.all_gather(out_weight, "req", axis_index_groups=planes)
-    else:
+    weights = out_weight
+    if out_weight.shape[2] % LANES:
+        planes = [[z * columns + c for c in range(columns)] for z in range(outer)]
         weights = lax.all_gather(out_weight, "req", axis=2, tiled=True, axis_index_groups=planes)
-    resid_line = lax.all_gather(resid_in, "req", axis_index_groups=lines)
-    per_group = outer // groups
-    resid_part = lax.dynamic_slice_in_dim(resid_line, (row % per_group) * width, width, 3)
-    resid_part = jnp.where(row // per_group == lane_index, resid_part, 0).reshape(
-        outer, models * step_count, width
+    spot = ((column * outer + row) * share) % LANES
+    own_targets = lax.dynamic_slice_in_dim(targets, lane_index * share, share, 0)
+    target_tile = jnp.broadcast_to(
+        lax.dynamic_update_slice_in_dim(jnp.zeros(LANES, jnp.int32), own_targets, spot, 0)[None, :],
+        (8, LANES),
     )
-    every_target = lax.all_gather(targets, "req").reshape(outer, columns, groups, share)
-    own_targets = lax.dynamic_index_in_dim(every_target, lane_index, 2, False)
-    local_ids = jnp.swapaxes(own_targets, 0, 1).reshape(1, tokens) - shard_index * vocab_part
-
-    gated = jnp.concatenate(
-        [
-            mixer_block(
-                gate_in[model_index],
-                mix_in[model_index],
-                keys_in[model_index],
-                step_in[model_index],
-                kernel_mix[model_index],
-                kernel_keys[model_index],
-                step_bias[model_index],
-                decay_rate[model_index],
-                skip_gain[model_index],
-                history_mix[model_index],
-                history_keys[model_index],
-                start_state[model_index],
-                lengths[0],
-                continued[0],
-            )
-            for model_index in range(models)
-        ]
-    )
+    skip_wide = jnp.repeat(skip_gain, inner_part // skip_gain.shape[1], axis=1)
+    requests, past = history_mix.shape[1:3]
+    history_rows = history_mix * continued[0].astype(jnp.bfloat16)[:, None, None]
+    history_rows = history_rows.astype(jnp.float32).reshape(models, requests * past, inner_part)
+    key_rows = history_keys * continued[0].astype(jnp.bfloat16)[:, None, None]
+    key_rows = key_rows.astype(jnp.float32).reshape(models, requests * past, keys_in.shape[2])
     rows = models * step_count
     line_rows = outer * share
     sends = outer - 1 + outer * (inner - 1) + outer * inner
     dma = pltpu.SemaphoreType.DMA
     vmem = pl.BlockSpec(memory_space=pltpu.VMEM)
+    smem = pl.BlockSpec(memory_space=pltpu.SMEM)
     anywhere = pl.BlockSpec(memory_space=pl.ANY)
     scores = pl.pallas_call(
         functools.partial(score_kernel, outer, inner, groups),
         out_shape=jax.ShapeDtypeStruct((models, LANES), jnp.float32),
-        in_specs=[vmem] * 5 + [anywhere] * 2,
+        in_specs=[vmem] * 15 + [smem] * 2 + [anywhere] * 3,
         out_specs=vmem,
         scratch_shapes=[
+            pltpu.VMEM(start_state.shape, jnp.bfloat16),
+            pltpu.VMEM((rows, inner_part), jnp.float32),
+            pltpu.VMEM((outer, models, step_count, width), jnp.bfloat16),
+            pltpu.VMEM((shards, 8, LANES), jnp.int32),
             pltpu.VMEM((models, inner_part, width), jnp.bfloat16),
             pltpu.VMEM((models, vocab_part, features), jnp.bfloat16),
             pltpu.VMEM((groups, rows, LANES), jnp.float32),
@@ -515,6 +701,13 @@
             pltpu.VMEM((models, tokens, features), jnp.bfloat16),
             pltpu.VMEM((tokens // LANES, 8, LANES), jnp.float32),
             pltpu.VMEM((shards, 8, LANES), jnp.float32),
+            dma,
+            dma((outer // groups,)),
+            dma((outer,)),
+            dma((shards,)),
+            dma((shards,)),
+            dma,
+            dma((2 * inner,)),
             dma((columns,)),
             dma((models,)),
             dma((groups,)),
@@ -531,8 +724,28 @@
         compiler_params=pltpu.CompilerParams(
             collective_id=0, has_side_effects=True, vmem_limit_bytes=50 * 1024 * 1024
         ),
-    )(gated, norm_gain, final_gain, resid_part, local_ids, weights, head_weight)
-    spot = ((column * outer + row) * share) % LANES
+    )(
+        gate_in,
+        mix_in,
+        keys_in,
+        step_in,
+        kernel_mix,
+        kernel_keys,
+        step_bias,
+        decay_rate,
+        skip_wide,
+        history_rows,
+        key_rows,
+        norm_gain,
+        final_gain,
+        resid_in,
+        target_tile,
+        lengths,
+        continued,
+        start_state,
+        weights,
+        head_weight,
+    )
     own_scores = lax.dynamic_slice_in_dim(scores, spot, share, 1)
     scored_rows = lax.dynamic_slice_in_dim(score_flag, lane_index * share, share, 0)
     return own_scores * scored_rows.astype(jnp.float32)[None, :]

time: 229 us -> 144 us (0.63)
  blocking collectives: 63.4 us -> 0 us
  matrix products: 21.6 us -> 0 us
  Pallas kernels: 107 us -> 127 us
  between operations: 15.2 us -> 0.07 us
  other arithmetic: 7.69 us -> 3.99 us
    unnamed x1 -> x0, blocking collectives: 63.4 us -> none
    dot_general x20 -> x0, matrix products: 21.6 us -> none  [the longest x2 10 us: mixer_block(): readings = jnp.einsum('tn,rcn->trc', readout, initial, precision=PRECISE)]
    pallas_call x1, Pallas kernels: 107 us -> 127 us  [local(): pl.pallas_call(functools.partial(score_kernel, outer, inner, groups), out...]
    unnamed x109 -> x27, local copies, waits for them, and re-layouts: 1.1 us -> 11.5 us
    slice x13 -> x0, local copies, waits for them, and re-layouts: 5.49 us -> none  [the longest x6 2.71 us: causal_conv(): current[:-lag_steps]]
  transfers between devices with their start and end apart: 2 -> 0, of which waited for: 0 -> 0; matrix products, arithmetic and copies ran while one was open for 18% -> 0% of each run, Pallas kernels for 0% -> 0%
where the time goes in v2:
time: 144 us
  Pallas kernels  127 us (88%)
  local copies, waits for them, and re-layouts  12.5 us (9%)
  other arithmetic  3.99 us (3%)
    pallas_call x1, Pallas kernels, local(): pl.pallas_call(functools.partial(score_kernel, outer, inner, groups), out...  127 us
    unnamed x27, local copies, waits for them, and re-layouts  11.5 us

profile of v2, /device:TPU:0, one launch (start us, length us, event | category | flops | bytes accessed | tf_op | source)
XLA Modules:
  0.0 143.7 jit_solution(11604856667486955542)
XLA Ops:
  0.0 0.8 dynamic-slice_convert_fusion
  0.8 0.7 convert_bitcast_fusion
  1.5 1.0 broadcast_multiply_fusion
  2.5 0.1 bitcast_convert_fusion
  2.6 0.1 copy.26.history_mix_ref
  2.7 0.8 broadcast_multiply_fusion.1
  3.5 0.8 broadcast_in_dim.6
  4.2 0.1 reshape.25.skip_ref
  4.3 0.8 copy.25.step_ref
  5.2 1.2 copy-done
  6.4 1.0 copy-done.1
  7.4 1.0 copy-done.2
  8.5 0.9 copy-done.3
  9.4 0.8 copy-done.4
  10.3 0.8 copy-done.5
  11.1 0.7 copy-done.6
  11.8 0.7 copy-done.7
  12.5 0.7 copy-done.8
  13.2 0.7 copy-done.9
  13.9 0.7 copy-done.10
  14.6 0.7 copy-done.11
  15.2 0.7 copy-done.12
  15.9 127.2 %shard_map.199 = f32[2,128]{1,0:T(2,128)S(1)} custom-call(bf16[2,64,2048]{2,1,0:T(8,128)(2,1)S(1)} %copy-done.1, bf16[2,64,2048]{2,1,0:T(8,128)(2,1)S(1)} %copy-done.2, bf16[2,64,256]{2,1,0:T(8,128)(2,1)S(1)} %copy-done.4, bf16[2,64,32]{2,1,0:T(8,128)(2,1)S(1)} %copy.25.step_ref, f32[2,4,2048]{2,1,0:T(4,128)S(1)} %copy-done.5, f32[2,4,256]{2,1,0:T(4,128)S(1)} %copy-done.8, ...), custom_call_target="tpu_custom_call" | custom-call | tf_op jit(solution)/shard_map/pallas_call | solution.py:683
  143.1 0.6 dynamic-slice_multiply_fusion
  (17 shorter events, 0.0 us)
Async XLA Ops:
  5.1 1.2 copy-start
  6.4 1.0 copy-start.1
  7.4 1.0 copy-start.2
  8.5 0.9 copy-start.3
  9.4 0.8 copy-start.4
  10.3 0.8 copy-start.5
  11.1 0.7 copy-start.6
  11.8 0.7 copy-start.7
  12.5 0.7 copy-start.8
  13.2 0.7 copy-start.9
  13.9 0.7 copy-start.10
  14.6 0.7 copy-start.11
  15.2 0.7 copy-start.12

commit v3 on v2

--- a/solution.py
+++ b/solution.py
@@ -73,10 +73,13 @@
     taps = kernel_mix_ref.shape[1]
     several = CHUNK // head_size
 
+    keeps = [continued_ref[0, request].astype(jnp.float32) for request in range(requests)]
+
     def rows_of(history_ref, spot):
         return [
             [
-                history_ref[model, pl.ds(request * (taps - 1) + slot, 1), spot]
+                history_ref[model, request, pl.ds(slot, 1), spot].astype(jnp.float32)
+                * keeps[request]
                 for slot in range(taps - 1)
             ]
             for request in range(requests)
@@ -105,8 +108,7 @@
     row_segment = segment[:, :states]
     by_request = []
     for request in range(requests):
-        keep = continued_ref[0, request].astype(jnp.float32)
-        part = jnp.where(row_segment == request, readout, 0.0) * keep
+        part = jnp.where(row_segment == request, readout, 0.0) * keeps[request]
         by_request.append(jnp.concatenate(halves(part), axis=0))
 
     square = (slots, slots)
@@ -122,7 +124,8 @@
     log_decay = -step_size * decay_rate_ref[pl.ds(model, 1), :]
     running = jnp.dot(causal, log_decay, precision=PRECISE, preferred_element_type=jnp.float32)
     carried = jnp.exp(jnp.minimum(running, 0.0))
-    per_head = jnp.concatenate([running, step_size, carried], axis=0)
+    skip = jnp.broadcast_to(skip_ref[pl.ds(model, 1), :], (8, heads))
+    per_head = jnp.concatenate([running, step_size, carried, skip], axis=0)
     strength = jnp.concatenate([causal * intersection] * several, axis=1)
     causal_wide = jnp.concatenate([causal] * several, axis=1)
     same_wide = jnp.concatenate([same] * several, axis=1)
@@ -158,7 +161,8 @@
         )
         run_to = spread_out[:slots]
         step_wide = spread_out[slots : 2 * slots]
-        carried_wide = spread_out[2 * slots :]
+        carried_wide = spread_out[2 * slots : 3 * slots]
+        skip_wide = spread_out[3 * slots : 3 * slots + 1]
         run_from = jnp.sum(run_to * same_wide, axis=0, keepdims=True)
         decay = jnp.exp(jnp.minimum(run_to - run_from, 0.0) * causal_wide)
         attend_high, attend_low = halves(decay * strength)
@@ -174,7 +178,7 @@
             term = dot_f32(by_request[request], state_ref[model, request, spot, :], ((1,), (1,)))
             readings = term if readings is None else readings + term
         chosen = readings[:slots] + readings[slots:]
-        output = output + carried_wide * chosen + skip_ref[pl.ds(model, 1), spot] * mixed
+        output = output + carried_wide * chosen + skip_wide * mixed
         gate = gate_ref[model, :, spot].astype(jnp.float32)
         gated[pl.ds(model * slots, slots), spot] = output * jax.nn.silu(gate)
         return 0
@@ -199,66 +203,49 @@
     return value
 
 
-def score_kernel(
-    outer,
-    inner,
-    groups,
-    gate_ref,
-    mix_ref,
-    keys_ref,
-    step_ref,
-    kernel_mix_ref,
-    kernel_keys_ref,
-    step_bias_ref,
-    decay_rate_ref,
-    skip_ref,
-    history_mix_ref,
-    history_keys_ref,
-    gain_ref,
-    final_gain_ref,
-    resid_ref,
-    target_ref,
-    lengths_ref,
-    continued_ref,
-    state_ref,
-    weight_ref,
-    head_ref,
-    result_ref,
-    state,
-    gated_ref,
-    resid,
-    targets_in,
-    weight,
-    head,
-    squares,
-    normed,
-    part,
-    landed,
-    total,
-    hidden,
-    final,
-    stats,
-    stats_in,
-    state_sem,
-    resid_send,
-    resid_recv,
-    target_send,
-    target_recv,
-    weight_sem,
-    weight_send,
-    weight_recv,
-    head_sem,
-    square_send,
-    square_recv,
-    normed_send,
-    normed_recv,
-    part_send,
-    part_recv,
-    hidden_send,
-    hidden_recv,
-    stats_send,
-    stats_recv,
-):
+def score_kernel(outer, inner, groups, operand_count, *refs):
+    operands, refs = refs[:operand_count], refs[operand_count:]
+    lengths_ref, continued_ref, state_ref, weight_ref, head_ref, result_ref = refs[:6]
+    copies, refs = refs[6 : 6 + operand_count], refs[6 + operand_count :]
+    mixer_copies, (gain_ref, final_gain_ref, resid_ref, target_ref) = copies[:-4], copies[-4:]
+    gate_ref = copies[0]
+    (
+        operand_sem,
+        state,
+        gated_ref,
+        resid,
+        targets_in,
+        weight,
+        head,
+        squares,
+        normed,
+        part,
+        landed,
+        total,
+        hidden,
+        final,
+        stats,
+        stats_in,
+        state_sem,
+        resid_send,
+        resid_recv,
+        target_send,
+        target_recv,
+        weight_sem,
+        weight_send,
+        weight_recv,
+        head_sem,
+        square_send,
+        square_recv,
+        normed_send,
+        normed_recv,
+        part_send,
+        part_recv,
+        hidden_send,
+        hidden_recv,
+        stats_send,
+        stats_recv,
+    ) = refs
     me = lax.axis_index("req")
     lane = lax.axis_index("tp")
     columns = inner * CORES
@@ -290,6 +277,12 @@
     def landing(buffer, recv_sem):
         pltpu.make_async_copy(buffer, buffer, recv_sem).wait()
 
+    loads = [
+        pltpu.make_async_copy(operand, copy, operand_sem.at[index])
+        for index, (operand, copy) in enumerate(zip(operands, copies))
+    ]
+    for load in loads:
+        load.start()
     barrier = pltpu.get_barrier_semaphore()
     for step in range(1, shards):
         pl.semaphore_signal(
@@ -325,6 +318,8 @@
     for load in head_loads:
         load.start()
 
+    for load in loads:
+        load.wait()
     pl.semaphore_wait(barrier, shards - 1 + groups - 1)
 
     def resid_copy(index):
@@ -366,64 +361,45 @@
             )
         targets_in[me] = target_ref[...]
 
-    with jax.named_scope("mixer"):
-        state_load.wait()
-        for model in range(models):
-            mixer(
-                model,
-                gate_ref,
-                mix_ref,
-                keys_ref,
-                step_ref,
-                kernel_mix_ref,
-                kernel_keys_ref,
-                step_bias_ref,
-                decay_rate_ref,
-                skip_ref,
-                history_mix_ref,
-                history_keys_ref,
-                state,
-                lengths_ref,
-                continued_ref,
-                gated_ref,
-            )
-
-    with jax.named_scope("gated_norm"):
-        for model in range(models):
+    def mix(model):
+        with jax.named_scope("mixer"):
+            mixer(model, *mixer_copies, state, lengths_ref, continued_ref, gated_ref)
             rows = pl.ds(model * slots, slots)
             values = gated_ref[rows, :]
             own = jnp.sum(values * values, axis=1, keepdims=True)
-            squares[lane, rows, :] = jnp.broadcast_to(own, (slots, LANES))
-        for step in range(1, groups):
-            send(
-                squares.at[lane],
-                squares.at[lane],
-                square_send.at[step],
-                square_recv.at[lane],
-                (me, lax.rem(lane + step, groups)),
-            )
-        for step in range(1, groups):
-            other = lax.rem(lane + step, groups)
-            landing(squares.at[other], square_recv.at[other])
-        for model in range(models):
+            squares[lane, model] = jnp.broadcast_to(own, (slots, LANES))
+            for step in range(1, groups):
+                send(
+                    squares.at[lane, model],
+                    squares.at[lane, model],
+                    square_send.at[step, model],
+                    square_recv.at[lane, model],
+                    (me, lax.rem(lane + step, groups)),
+                )
+
+    def gated_norm(model):
+        with jax.named_scope("gated_norm"):
+            for step in range(1, groups):
+                other = lax.rem(lane + step, groups)
+                landing(squares.at[other, model], square_recv.at[other, model])
             rows = pl.ds(model * slots, slots)
-            level = squares[0, rows, 0:1]
+            level = squares[0, model, :, 0:1]
             for group in range(1, groups):
-                level = level + squares[group, rows, 0:1]
+                level = level + squares[group, model, :, 0:1]
             scale = lax.rsqrt(level / (inner_part * groups) + EPSILON)
-            normed[row, rows, :] = (
+            normed[model, row] = (
                 gated_ref[rows, :] * scale * gain_ref[model : model + 1, :]
             ).astype(jnp.bfloat16)
-
-    with jax.named_scope("out_projection"):
-        for mask in range(1, outer):
-            send(
-                normed.at[row],
-                normed.at[row],
-                normed_send.at[mask],
-                normed_recv.at[row],
-                (flipped(row, mask) * columns + column, lane),
-            )
+            for mask in range(1, outer):
+                send(
+                    normed.at[model, row],
+                    normed.at[model, row],
+                    normed_send.at[model, mask],
+                    normed_recv.at[model, row],
+                    (flipped(row, mask) * columns + column, lane),
+                )
+
+    def pass_weights():
         weight_load.wait()
         if exchanged:
             for side in range(1, inner):
@@ -457,112 +433,104 @@
             for side in range(inner):
                 other = flipped(x, side) * CORES + sibling
                 landing(columns_of(other), weight_recv.at[other])
-        for mask in range(outer):
-            line = flipped(row, mask)
-            if mask:
-                landing(normed.at[line], normed_recv.at[line])
-            for model in range(models):
-                rows = pl.ds(model * slots, slots)
+
+    def project(model):
+        with jax.named_scope("out_projection"):
+            for mask in range(outer):
+                line = flipped(row, mask)
+                if mask:
+                    landing(normed.at[model, line], normed_recv.at[model, line])
                 product = jnp.dot(
-                    normed[line, rows, :], weight[model], preferred_element_type=jnp.float32
+                    normed[model, line], weight[model], preferred_element_type=jnp.float32
                 ) + resid[line, model].astype(jnp.float32)
                 for group in range(groups):
-                    part[group, line, pl.ds(model * share, share), :] = product[
-                        group * share : (group + 1) * share
-                    ]
-            for step in range(1, groups):
-                other = lax.rem(lane + step, groups)
-                send(
-                    part.at[other, line],
-                    landed.at[lane, line],
-                    part_send.at[step, mask],
-                    part_recv.at[lane, line],
-                    (me, other),
-                )
-        for mask in range(outer):
-            line = flipped(row, mask)
-            summed = part[lane, line]
-            for step in range(1, groups):
-                other = lax.rem(lane + step, groups)
-                landing(landed.at[other, line], part_recv.at[other, line])
-                summed = summed + landed[other, line]
-            for model in range(models):
-                start = pl.multiple_of(model * line_rows + line * share, share)
-                total[pl.ds(start, share), :] = summed[model * share : (model + 1) * share]
-        hidden[row, column] = total[...].astype(jnp.bfloat16)
-
-    def normalize(source):
+                    part[group, model, line] = product[group * share : (group + 1) * share]
+                for step in range(1, groups):
+                    other = lax.rem(lane + step, groups)
+                    send(
+                        part.at[other, model, line],
+                        landed.at[lane, model, line],
+                        part_send.at[step, model, mask],
+                        part_recv.at[lane, model, line],
+                        (me, other),
+                    )
+
+    def pass_on(model, line, source, device):
+        send(
+            hidden.at[model, line, source],
+            hidden.at[model, line, source],
+            hidden_send.at[model, next(counters[model])],
+            hidden_recv.at[model, line, source],
+            (device, lane),
+        )
+
+    def reduce(model):
+        with jax.named_scope("reduce_groups"):
+            for mask in range(outer):
+                line = flipped(row, mask)
+                summed = part[lane, model, line]
+                for step in range(1, groups):
+                    other = lax.rem(lane + step, groups)
+                    landing(landed.at[other, model, line], part_recv.at[other, model, line])
+                    summed = summed + landed[other, model, line]
+                total[pl.ds(pl.multiple_of(line * share, share), share), :] = summed
+            hidden[model, row, column] = total[...].astype(jnp.bfloat16)
+            for mask in range(1, outer):
+                pass_on(model, row, column, flipped(row, mask) * columns + column)
+
+    def normalize(model, source):
         level = None
         for line in range(outer):
-            values = hidden[line, source].astype(jnp.float32)
+            values = hidden[model, line, source].astype(jnp.float32)
             own = jnp.sum(values * values, axis=1, keepdims=True)
             level = own if level is None else level + own
         scale = lax.rsqrt(level / features + EPSILON)
         start = pl.multiple_of(source * line_rows, line_rows)
         for line in range(outer):
-            for model in range(models):
-                rows = slice(model * line_rows, (model + 1) * line_rows)
-                values = hidden[line, source, rows, :].astype(jnp.float32)
-                spot = slice(line * width, (line + 1) * width)
-                final[model, pl.ds(start, line_rows), spot] = (
-                    values * scale[rows] * final_gain_ref[model : model + 1, spot]
-                ).astype(jnp.bfloat16)
-
-    with jax.named_scope("gather_features"):
-        counter = iter(range(hidden_send.shape[0]))
-
-        def pass_on(line, source, device):
-            send(
-                hidden.at[line, source],
-                hidden.at[line, source],
-                hidden_send.at[next(counter)],
-                hidden_recv.at[line, source],
-                (device, lane),
-            )
-
-        for mask in range(1, outer):
-            pass_on(row, column, flipped(row, mask) * columns + column)
+            values = hidden[model, line, source].astype(jnp.float32)
+            spot = slice(line * width, (line + 1) * width)
+            final[model, pl.ds(start, line_rows), spot] = (
+                values * scale * final_gain_ref[model : model + 1, spot]
+            ).astype(jnp.bfloat16)
+
+    def arrived(model, line, source):
+        landing(hidden.at[model, line, source], hidden_recv.at[model, line, source])
+
+    def pass_line(model):
         for mask in range(outer):
             line = flipped(row, mask)
             if mask:
-                landing(hidden.at[line, column], hidden_recv.at[line, column])
+                arrived(model, line, column)
             for side in range(1, inner):
-                pass_on(line, column, row * columns + flipped(x, side) * CORES + core)
-            pass_on(line, column, row * columns + x * CORES + sibling)
-        normalize(column)
+                pass_on(model, line, column, row * columns + flipped(x, side) * CORES + core)
+            pass_on(model, line, column, row * columns + x * CORES + sibling)
+        normalize(model, column)
+
+    def pass_plane(model):
         for side in range(1, inner):
             source = flipped(x, side) * CORES + core
             for mask in range(outer):
                 line = flipped(row, mask)
-                landing(hidden.at[line, source], hidden_recv.at[line, source])
-                pass_on(line, source, row * columns + x * CORES + sibling)
-            normalize(source)
+                arrived(model, line, source)
+                pass_on(model, line, source, row * columns + x * CORES + sibling)
+            normalize(model, source)
+
+    def collect(model):
         for side in range(inner):
             source = flipped(x, side) * CORES + sibling
             for mask in range(outer):
-                line = flipped(row, mask)
-                landing(hidden.at[line, source], hidden_recv.at[line, source])
-            normalize(source)
-
-    with jax.named_scope("head"):
-        entries = head_ref.shape[1]
-        tile = max(size for size in range(16, 401, 16) if entries % size == 0)
-        tokens = final.shape[1]
-        stats[...] = jnp.zeros_like(stats)
-        for step in range(1, shards):
-            other = lax.rem(me + step, shards)
-            landing(targets_in.at[other], target_recv.at[other])
-        tiles = [None] * (tokens // LANES)
-        for source in range(columns):
-            for line in range(outer):
-                index = ((source * outer + line) * share) // LANES
-                term = targets_in[line * columns + source, 0:1, :]
-                tiles[index] = term if tiles[index] is None else tiles[index] + term
-        local_ids = jnp.concatenate(tiles, axis=1) - me * entries
-        for model in range(models):
+                arrived(model, flipped(row, mask), source)
+            normalize(model, source)
+
+    entries = head_ref.shape[1]
+    tile = max(size for size in range(16, 401, 16) if entries % size == 0)
+    tokens = final.shape[1]
+
+    def score(model, local_ids):
+        with jax.named_scope("head"):
             head_loads[model].wait()
 
-            def scan(index, state, model=model):
+            def scan(index, state):
                 peak, spread, picked = state
                 start = pl.multiple_of(index * tile, tile)
                 logits = lax.dot_general(
@@ -588,6 +556,36 @@
                     stats[index, pl.ds(3 * model + kind, 1), :] = found[kind][
                         :, index * LANES : (index + 1) * LANES
                     ]
+
+    counters = [iter(range(hidden_send.shape[1])) for _ in range(models)]
+    state_load.wait()
+    for model in range(models):
+        mix(model)
+        gated_norm(model)
+    pass_weights()
+    stats[...] = jnp.zeros_like(stats)
+    for step in range(1, shards):
+        other = lax.rem(me + step, shards)
+        landing(targets_in.at[other], target_recv.at[other])
+    tiles = [None] * (tokens // LANES)
+    for source in range(columns):
+        for line in range(outer):
+            index = ((source * outer + line) * share) // LANES
+            term = targets_in[line * columns + source, 0:1, :]
+            tiles[index] = term if tiles[index] is None else tiles[index] + term
+    local_ids = jnp.concatenate(tiles, axis=1) - me * entries
+    for model in range(models):
+        project(model)
+        reduce(model)
+    pass_line(0)
+    pass_plane(0)
+    for model in range(1, models):
+        pass_line(model)
+        collect(model - 1)
+        score(model - 1, local_ids)
+        pass_plane(model)
+    collect(models - 1)
+    score(models - 1, local_ids)
 
     with jax.named_scope("merge"):
 
@@ -667,12 +665,6 @@
         lax.dynamic_update_slice_in_dim(jnp.zeros(LANES, jnp.int32), own_targets, spot, 0)[None, :],
         (8, LANES),
     )
-    skip_wide = jnp.repeat(skip_gain, inner_part // skip_gain.shape[1], axis=1)
-    requests, past = history_mix.shape[1:3]
-    history_rows = history_mix * continued[0].astype(jnp.bfloat16)[:, None, None]
-    history_rows = history_rows.astype(jnp.float32).reshape(models, requests * past, inner_part)
-    key_rows = history_keys * continued[0].astype(jnp.bfloat16)[:, None, None]
-    key_rows = key_rows.astype(jnp.float32).reshape(models, requests * past, keys_in.shape[2])
     rows = models * step_count
     line_rows = outer * share
     sends = outer - 1 + outer * (inner - 1) + outer * inner
@@ -680,24 +672,43 @@
     vmem = pl.BlockSpec(memory_space=pltpu.VMEM)
     smem = pl.BlockSpec(memory_space=pltpu.SMEM)
     anywhere = pl.BlockSpec(memory_space=pl.ANY)
+    operands = (
+        gate_in,
+        mix_in,
+        keys_in,
+        step_in,
+        kernel_mix,
+        kernel_keys,
+        step_bias,
+        decay_rate,
+        skip_gain,
+        history_mix,
+        history_keys,
+        norm_gain,
+        final_gain,
+        resid_in,
+        target_tile,
+    )
     scores = pl.pallas_call(
-        functools.partial(score_kernel, outer, inner, groups),
+        functools.partial(score_kernel, outer, inner, groups, len(operands)),
         out_shape=jax.ShapeDtypeStruct((models, LANES), jnp.float32),
-        in_specs=[vmem] * 15 + [smem] * 2 + [anywhere] * 3,
+        in_specs=[anywhere] * len(operands) + [smem] * 2 + [anywhere] * 3,
         out_specs=vmem,
-        scratch_shapes=[
+        scratch_shapes=[pltpu.VMEM(operand.shape, operand.dtype) for operand in operands]
+        + [
+            dma((len(operands),)),
             pltpu.VMEM(start_state.shape, jnp.bfloat16),
             pltpu.VMEM((rows, inner_part), jnp.float32),
             pltpu.VMEM((outer, models, step_count, width), jnp.bfloat16),
             pltpu.VMEM((shards, 8, LANES), jnp.int32),
             pltpu.VMEM((models, inner_part, width), jnp.bfloat16),
             pltpu.VMEM((models, vocab_part, features), jnp.bfloat16),
-            pltpu.VMEM((groups, rows, LANES), jnp.float32),
-            pltpu.VMEM((outer, rows, inner_part), jnp.bfloat16),
-            pltpu.VMEM((groups, outer, models * share, width), jnp.float32),
-            pltpu.VMEM((groups, outer, models * share, width), jnp.float32),
-            pltpu.VMEM((models * line_rows, width), jnp.float32),
-            pltpu.VMEM((outer, columns, models * line_rows, width), jnp.bfloat16),
+            pltpu.VMEM((groups, models, step_count, LANES), jnp.float32),
+            pltpu.VMEM((models, outer, step_count, inner_part), jnp.bfloat16),
+            pltpu.VMEM((groups, models, outer, share, width), jnp.float32),
+            pltpu.VMEM((groups, models, outer, share, width), jnp.float32),
+            pltpu.VMEM((line_rows, width), jnp.float32),
+            pltpu.VMEM((models, outer, columns, line_rows, width), jnp.bfloat16),
             pltpu.VMEM((models, tokens, features), jnp.bfloat16),
             pltpu.VMEM((tokens // LANES, 8, LANES), jnp.float32),
             pltpu.VMEM((shards, 8, LANES), jnp.float32),
@@ -710,42 +721,21 @@
             dma((2 * inner,)),
             dma((columns,)),
             dma((models,)),
-            dma((groups,)),
-            dma((groups,)),
-            dma((outer,)),
-            dma((outer,)),
-            dma((groups, outer)),
-            dma((groups, outer)),
-            dma((sends,)),
-            dma((outer, columns)),
+            dma((groups, models)),
+            dma((groups, models)),
+            dma((models, outer)),
+            dma((models, outer)),
+            dma((groups, models, outer)),
+            dma((groups, models, outer)),
+            dma((models, sends)),
+            dma((models, outer, columns)),
             dma((shards,)),
             dma((shards,)),
         ],
         compiler_params=pltpu.CompilerParams(
             collective_id=0, has_side_effects=True, vmem_limit_bytes=50 * 1024 * 1024
         ),
-    )(
-        gate_in,
-        mix_in,
-        keys_in,
-        step_in,
-        kernel_mix,
-        kernel_keys,
-        step_bias,
-        decay_rate,
-        skip_wide,
-        history_rows,
-        key_rows,
-        norm_gain,
-        final_gain,
-        resid_in,
-        target_tile,
-        lengths,
-        continued,
-        start_state,
-        weights,
-        head_weight,
-    )
+    )(*operands, lengths, continued, start_state, weights, head_weight)
     own_scores = lax.dynamic_slice_in_dim(scores, spot, share, 1)
     scored_rows = lax.dynamic_slice_in_dim(score_flag, lane_index * share, share, 0)
     return own_scores * scored_rows.astype(jnp.float32)[None, :]

time: 144 us -> 127 us (0.88)
  Pallas kernels: 127 us -> 111 us
  other arithmetic: 3.99 us -> 1.46 us
    pallas_call x1, Pallas kernels: 127 us -> 111 us  [local(): pl.pallas_call(functools.partial(score_kernel, outer, inner, groups, len(...]
    unnamed x27 -> x31, local copies, waits for them, and re-layouts: 11.5 us -> 13.9 us
    mul x2 -> x0, other arithmetic: 1.79 us -> none  [the longest x1 1.01 us: local(): history_mix * continued[0].astype(jnp.bfloat16)[:, None, None]]
where the time goes in v3:
time: 127 us
  Pallas kernels  111 us (87%)
  local copies, waits for them, and re-layouts  13.9 us (11%)
  other arithmetic  1.46 us (1%)
    pallas_call x1, Pallas kernels, local(): pl.pallas_call(functools.partial(score_kernel, outer, inner, groups, len(...  111 us
    unnamed x31, local copies, waits for them, and re-layouts  13.9 us

profile of v3, /device:TPU:0, one launch (start us, length us, event | category | flops | bytes accessed | tf_op | source)
XLA Modules:
  0.0 126.6 jit_solution(13051292061848114786)
XLA Ops:
  0.0 0.8 dynamic-slice_convert_fusion
  0.8 0.7 copy.24.refs_10_
  1.5 0.8 copy.22.refs_3_
  2.3 0.9 copy.23.refs_9_
  3.3 0.0 copy-start
  3.3 1.2 copy-done
  4.5 0.0 copy-start.1
  4.5 1.0 copy-done.1
  5.6 0.0 copy-start.2
  5.6 1.0 copy-done.2
  6.6 0.0 copy-start.3
  6.6 0.9 copy-done.3
  7.6 0.8 copy-done.4
  8.4 0.8 copy-done.5
  9.2 0.7 copy-done.6
  10.0 0.7 copy-done.7
  10.7 0.7 copy-done.8
  11.4 0.7 copy-done.9
  12.0 0.7 copy-done.10
  12.7 0.7 copy-done.11
  13.4 0.7 copy-done.12
  14.1 0.7 copy-done.13
  14.7 111.3 %shard_map.199 = f32[2,128]{1,0:T(2,128)S(1)} custom-call(bf16[2,64,2048]{2,1,0:T(8,128)(2,1)S(1)} %copy-done.1, bf16[2,64,2048]{2,1,0:T(8,128)(2,1)S(1)} %copy-done.2, bf16[2,64,256]{2,1,0:T(8,128)(2,1)S(1)} %copy-done.4, bf16[2,64,32]{2,1,0:T(8,128)(2,1)S(1)} %copy.22.refs_3_, f32[2,4,2048]{2,1,0:T(4,128)S(1)} %copy-done.5, f32[2,4,256]{2,1,0:T(4,128)S(1)} %copy-done.8, ...), custom_call_target="tpu_custom_call" | custom-call | tf_op jit(solution)/shard_map/pallas_call | solution.py:692
  126.0 0.6 dynamic-slice_multiply_fusion
  (12 shorter events, 0.0 us)
Async XLA Ops:
  3.3 1.2 copy-start
  4.5 1.0 copy-start.1
  5.6 1.0 copy-start.2
  6.6 0.9 copy-start.3
  7.6 0.8 copy-start.4
  8.4 0.8 copy-start.5
  9.2 0.7 copy-start.6
  9.9 0.7 copy-start.7
  10.7 0.7 copy-start.8
  11.4 0.7 copy-start.9
  12.0 0.7 copy-start.10
  12.7 0.7 copy-start.11
  13.4 0.7 copy-start.12
  14.1 0.7 copy-start.13
